TPU v7x, 32 devices: a whole 2x2x4 slice. The times are simulated.
32 devices in a mesh: dp: 4 (over y, x), modes: 8 (over z, core).
Axes of the slice: x: 2, y: 2, z: 4, core: 2. Of those that a mesh axis runs over, the one named last changes fastest.
Arguments:
- patches: bfloat16 [4, 4, 8, 512, 768], P(None, 'dp', 'modes'), may hold values from -6 to 6
- cotangent: bfloat16 [4, 4, 8, 512, 768], P(None, 'dp', 'modes'), may hold values from -6 to 6
- heights: int32 [4, 4], P(None, 'dp'), may hold values from 2 to 8, as said below
- widths: int32 [4, 4], P(None, 'dp'), may hold values from 256 to 512, as said below
- band_lengths: int32 [8], replicated, may hold values from 1 to 64, as said below
- dense_master: float32 [3072, 2, 768], P(('dp', 'modes'))
- dense_first: float32 [3072, 2, 768], P(('dp', 'modes')), may hold values from -0.00030517578 to 0.00030517578
- dense_second: float32 [3072, 2, 768], P(('dp', 'modes')), may hold values from 5.1756865e-09 to 8.360725e-08
- spectral_master: float32 [2, 2, 8, 96, 96], replicated, may hold values from -0.4375 to 0.4375
- spectral_first: float32 [2, 2, 8, 96, 96], replicated, may hold values from -0.00030517578 to 0.00030517578
- spectral_second: float32 [2, 2, 8, 96, 96], replicated, may hold values from 5.1756865e-09 to 8.360725e-08
- vector_master: float32 [13, 768], replicated, may hold values from -1 to 2
- vector_first: float32 [13, 768], replicated, may hold values from -0.0008544922 to 0.0008544922
- vector_second: float32 [13, 768], replicated, may hold values from 4.5784923e-08 to 7.564465e-07
Outputs:
- output: bfloat16 [4, 4, 8, 512, 768], P(None, 'dp', 'modes')
- input_grad: bfloat16 [4, 4, 8, 512, 768], P(None, 'dp', 'modes')
- grad_norm: float32 [], replicated
- dense_grad: float32 [3072, 2, 768], P(('dp', 'modes'))
- dense_new: float32 [3072, 2, 768], P(('dp', 'modes'))
- dense_first_new: float32 [3072, 2, 768], P(('dp', 'modes'))
- dense_second_new: float32 [3072, 2, 768], P(('dp', 'modes'))
- spectral_grad: float32 [2, 2, 8, 96, 96], replicated
- spectral_new: float32 [2, 2, 8, 96, 96], replicated
- spectral_first_new: float32 [2, 2, 8, 96, 96], replicated
- spectral_second_new: float32 [2, 2, 8, 96, 96], replicated
- vector_grad: float32 [13, 768], replicated
- vector_new: float32 [13, 768], replicated
- vector_first_new: float32 [13, 768], replicated
- vector_second_new: float32 [13, 768], replicated
Inputs may be any that keep to these rules, and one draw needn't show every extreme that they name: `heights`: among the entries of one index of dp over all micro-batches, one is exactly 8. `widths`: among the entries of one index of dp over all micro-batches, one is exactly 512. `band_lengths`: band j holds the wavenumbers from the sum of the earlier lengths on; one length is exactly 64; the lengths may add up to more than 256 or to less.
All inputs are finite; a program needn't handle non-finite values.
Results may differ from a plain program's by a relative error of at most 0.015.
The roundings to bfloat16 on the way count: a program that leaves them out, or rounds other values in their place, can miss the bound.
Values may be sent and summed in bfloat16 or wider, within the bound.
No kernel may reach another device: no remote copies, remote signals or barrier semaphores. Data moves between devices by JAX's collectives and lax.ppermute only.
A program may use at most 384 MiB of HBM per device.

v0:
```python
import math

import jax
import jax.numpy as jnp
from jax import lax
from jax.sharding import PartitionSpec as P

NB = 8
BS = 96
STEP = 10


SHRINK_LEVEL = 0.01
NORM_EPS = 1e-05
CLIP_LEVEL = 1.0
BETA_FIRST = 0.9
BETA_SECOND = 0.95
ADAM_EPS = 1e-08
RATE_MATRIX = 0.05
RATE_VECTOR = 0.5
DECAY_MATRIX = 0.1


def wave_table(wavenumbers, length, factors):
    positions = jnp.arange(length, dtype=jnp.int32)
    phase_int = wavenumbers[:, None] * positions[None, :] % length
    angles = phase_int.astype(jnp.float32) * (2.0 * math.pi / length)
    return jnp.stack([jnp.cos(angles) * factors[:, None], -jnp.sin(angles) * factors[:, None]])


def row_tables(length):
    row_index = jnp.arange(length, dtype=jnp.int32)
    phase_int = row_index[:, None] * row_index[None, :] % length
    angles = phase_int.astype(jnp.float32) * (2.0 * math.pi / length)
    cosine = jnp.cos(angles)
    sines = jnp.sin(angles)
    forward = jnp.stack([jnp.stack([cosine, sines], axis=1), jnp.stack([-sines, cosine], axis=1)])
    inverse = jnp.stack([jnp.stack([cosine, -sines], axis=1), jnp.stack([sines, cosine], axis=1)])
    return (forward, inverse)


def complex_matrix(weights):
    return jnp.stack([jnp.stack([weights[0], weights[1]]), jnp.stack([-weights[1], weights[0]])])


def fold_complex(grad_matrix):
    return jnp.stack([grad_matrix[0, 0] + grad_matrix[1, 1], grad_matrix[0, 1] - grad_matrix[1, 0]])


def split_blocks(values):
    return values.reshape(values.shape[:-1] + (NB, BS))


def block_mix(values, matrix):
    mixed = jnp.einsum(
        "ckpsni,pqnij->ckqsnj", split_blocks(values), matrix, preferred_element_type=jnp.float32
    )
    return mixed.reshape(values.shape)


def shrink(values):
    return values - SHRINK_LEVEL * jnp.tanh(values / SHRINK_LEVEL)


def norm_forward(values, gain_row, shift_row):
    centered = values - jnp.mean(values, axis=-1, keepdims=True)
    factor = lax.rsqrt(jnp.mean(centered * centered, axis=-1, keepdims=True) + NORM_EPS)
    unit_rows = centered * factor
    return (unit_rows * gain_row + shift_row, unit_rows, factor)


def norm_backward(grad_rows, unit_rows, factor, gain_row):
    scaled = grad_rows * gain_row
    return factor * (
        scaled
        - jnp.mean(scaled, axis=-1, keepdims=True)
        - unit_rows * jnp.mean(scaled * unit_rows, axis=-1, keepdims=True)
    )


def adam_update(master, first_old, second_old, gradient, rate, decay):
    first_new = BETA_FIRST * first_old + (1.0 - BETA_FIRST) * gradient
    second_new = BETA_SECOND * second_old + (1.0 - BETA_SECOND) * gradient * gradient
    moved = (
        first_new
        / (1.0 - BETA_FIRST**STEP)
        / (jnp.sqrt(second_new / (1.0 - BETA_SECOND**STEP)) + ADAM_EPS)
    )
    return (master - rate * (moved + decay * master), first_new, second_new)


def fetch_dense(dense_master):
    return lax.all_gather(dense_master.astype(jnp.bfloat16), ("dp", "modes"), axis=0, tiled=True)


def on_device(
    patches,
    cotangent,
    heights,
    widths,
    band_lengths,
    dense_master,
    dense_first,
    dense_second,
    spectral_master,
    spectral_first,
    spectral_second,
    vector_master,
    vector_first,
    vector_second,
):
    band_count = lax.axis_size("modes")
    my_band = lax.axis_index("modes")
    crop_count = patches.shape[1]
    row_cells = patches.shape[3]
    features = patches.shape[4]
    wave_count = row_cells // 2
    slot_count = 2 * wave_count // band_count
    ortho_scale = (band_count * row_cells) ** (-0.5)
    band_ends = jnp.cumsum(band_lengths)
    starts = band_ends - band_lengths
    kept_count = jnp.minimum(band_ends[-1], wave_count)
    offsets = jnp.arange(slot_count, dtype=jnp.int32)
    slot_waves = starts[:, None] + offsets[None, :]
    slot_valid = (offsets[None, :] < band_lengths[:, None]) & (slot_waves < kept_count)
    flat_waves = jnp.where(slot_valid, slot_waves, 0).reshape(-1)
    flat_valid = slot_valid.reshape(-1).astype(jnp.float32)
    forward_table = wave_table(flat_waves, row_cells, flat_valid * ortho_scale).astype(jnp.bfloat16)
    inverse_table = wave_table(
        flat_waves,
        row_cells,
        flat_valid * jnp.where(flat_waves == 0, ortho_scale, 2.0 * ortho_scale),
    ).astype(jnp.bfloat16)
    row_forward, row_inverse = row_tables(band_count)
    row_forward = row_forward.astype(jnp.bfloat16)
    row_inverse = row_inverse.astype(jnp.bfloat16)
    mine = jnp.arange(band_count, dtype=jnp.int32) == my_band
    my_keep = jnp.any(slot_valid & mine[:, None], axis=0).astype(jnp.float32)
    keep_shape = my_keep[None, None, None, :, None]
    spectral_low = spectral_master.astype(jnp.bfloat16)
    mix_first = complex_matrix(spectral_low[0])
    mix_second = complex_matrix(spectral_low[1])
    gain_one, shift_one = (vector_master[0], vector_master[1])
    gain_two, shift_two = (vector_master[2], vector_master[3])
    bias_first = vector_master[4:6][None, None, :, None, :]
    bias_second = vector_master[6:8][None, None, :, None, :]
    out_bias = vector_master[8]
    hidden_bias = vector_master[9:13].reshape(-1)
    dense_grad = jnp.zeros(dense_master.shape, jnp.float32)
    spectral_acc = jnp.zeros(spectral_master.shape, jnp.float32)
    vector_acc = jnp.zeros(vector_master.shape, jnp.float32)
    outputs = []
    input_grads = []
    for micro_index in range(patches.shape[0]):
        gathered = fetch_dense(dense_master)
        weight_up = gathered[:, 0, :]
        weight_down = gathered[:, 1, :]
        rows_ok = my_band < heights[micro_index]
        cols_ok = jnp.arange(row_cells, dtype=jnp.int32)[None, :] < widths[micro_index][:, None]
        cell_mask = (rows_ok[:, None] & cols_ok).astype(jnp.float32)[:, None, :, None]
        masked_in = patches[micro_index].astype(jnp.float32) * cell_mask
        normed_pre, unit_one, factor_one = norm_forward(masked_in, gain_one, shift_one)
        normed = normed_pre * cell_mask
        narrow = normed.astype(jnp.bfloat16)
        wave_rows = jnp.einsum(
            "pjw,crwd->crpjd", forward_table, narrow, preferred_element_type=jnp.float32
        )
        to_owner = wave_rows.astype(jnp.bfloat16).reshape(
            crop_count, 1, 2, band_count, slot_count, features
        )
        received = lax.all_to_all(to_owner, "modes", split_axis=3, concat_axis=1, tiled=True)
        item_count = received.shape[0]
        rows_in = received.reshape(item_count, band_count, 2, slot_count, features)
        mode_rows = jnp.einsum(
            "pjqh,chqsd->cjpsd", row_forward, rows_in, preferred_element_type=jnp.float32
        )
        mode_rows = mode_rows.astype(jnp.bfloat16)
        pre_active = block_mix(mode_rows, mix_first) + bias_first
        active = jax.nn.gelu(pre_active).astype(jnp.bfloat16)
        pre_shrink = block_mix(active, mix_second) + bias_second
        shrunk = (shrink(pre_shrink) * keep_shape).astype(jnp.bfloat16)
        back_rows = jnp.einsum(
            "phqj,cjqsd->chpsd", row_inverse, shrunk, preferred_element_type=jnp.float32
        )
        back_rows = back_rows.astype(jnp.bfloat16).reshape(
            item_count, band_count, 2, 1, slot_count, features
        )
        returned = lax.all_to_all(back_rows, "modes", split_axis=1, concat_axis=3, tiled=True)
        returned, mode_rows, pre_active, pre_shrink = (returned, mode_rows, pre_active, pre_shrink)
        back_flat = returned.reshape(crop_count, 1, 2, band_count * slot_count, features)
        filtered = jnp.einsum(
            "pjw,crpjd->crwd", inverse_table, back_flat, preferred_element_type=jnp.float32
        )
        middle = masked_in + normed + filtered
        normed_two, unit_two, factor_two = norm_forward(middle, gain_two, shift_two)
        tokens_low = normed_two.reshape(-1, features).astype(jnp.bfloat16)
        upper_in = (
            jnp.einsum("td,fd->tf", tokens_low, weight_up, preferred_element_type=jnp.float32)
            + hidden_bias
        )
        upper_value, gelu_pull = jax.vjp(jax.nn.gelu, upper_in)
        hidden = upper_value.astype(jnp.bfloat16)
        lower_out = jnp.dot(hidden, weight_down, preferred_element_type=jnp.float32) + out_bias
        output = (middle.reshape(-1, features) + lower_out).reshape(middle.shape) * cell_mask
        outputs.append(output.astype(jnp.bfloat16))
        grad_out = cotangent[micro_index].astype(jnp.float32) * cell_mask
        grad_flat = grad_out.reshape(-1, features)
        grad_low = grad_flat.astype(jnp.bfloat16)
        grad_hidden = jnp.einsum(
            "td,fd->tf", grad_low, weight_down, preferred_element_type=jnp.float32
        )
        grad_upper = gelu_pull(grad_hidden)[0]
        upper_low = grad_upper.astype(jnp.bfloat16)
        grad_tokens = jnp.dot(upper_low, weight_up, preferred_element_type=jnp.float32).reshape(
            middle.shape
        )
        grad_middle = grad_out + norm_backward(grad_tokens, unit_two, factor_two, gain_two)
        up_grad = jnp.einsum("tf,td->fd", upper_low, tokens_low, preferred_element_type=jnp.float32)
        down_grad = jnp.einsum("tf,td->fd", hidden, grad_low, preferred_element_type=jnp.float32)
        dense_grad = dense_grad + lax.psum_scatter(
            jnp.stack([up_grad, down_grad], axis=1),
            ("dp", "modes"),
            scatter_dimension=0,
            tiled=True,
        )
        filter_low = grad_middle.astype(jnp.bfloat16)
        grad_back = jnp.einsum(
            "pjw,crwd->crpjd", inverse_table, filter_low, preferred_element_type=jnp.float32
        )
        grad_back = grad_back.astype(jnp.bfloat16).reshape(
            crop_count, 1, 2, band_count, slot_count, features
        )
        grad_received = lax.all_to_all(grad_back, "modes", split_axis=3, concat_axis=1, tiled=True)
        grad_received = grad_received.reshape(crop_count, band_count, 2, slot_count, features)
        grad_shrunk = jnp.einsum(
            "phqj,chpsd->cjqsd", row_inverse, grad_received, preferred_element_type=jnp.float32
        )
        shrink_value, shrink_pull = jax.vjp(shrink, pre_shrink)
        grad_shrink = shrink_pull(grad_shrunk * keep_shape)[0]
        shrink_low = grad_shrink.astype(jnp.bfloat16)
        active_value, active_pull = jax.vjp(jax.nn.gelu, pre_active)
        active = active_value.astype(jnp.bfloat16)
        grad_mix_second = jnp.einsum(
            "chpsni,chqsnm->pqnim",
            split_blocks(active),
            split_blocks(shrink_low),
            preferred_element_type=jnp.float32,
        )
        grad_active = jnp.einsum(
            "cjqsnk,pqnik->cjpsni",
            split_blocks(shrink_low),
            mix_second,
            preferred_element_type=jnp.float32,
        ).reshape(pre_active.shape)
        grad_first = active_pull(grad_active)[0]
        first_low = grad_first.astype(jnp.bfloat16)
        grad_mix_first = jnp.einsum(
            "chpsni,chqsnm->pqnim",
            split_blocks(mode_rows),
            split_blocks(first_low),
            preferred_element_type=jnp.float32,
        )
        grad_modes = jnp.einsum(
            "cjqsnk,pqnik->cjpsni",
            split_blocks(first_low),
            mix_first,
            preferred_element_type=jnp.float32,
        ).reshape(pre_active.shape)
        grad_modes = grad_modes.astype(jnp.bfloat16)
        grad_rows = jnp.einsum(
            "pjqh,cjpsd->chqsd", row_forward, grad_modes, preferred_element_type=jnp.float32
        )
        grad_rows = grad_rows.astype(jnp.bfloat16).reshape(
            crop_count, band_count, 2, 1, slot_count, features
        )
        grad_spread = lax.all_to_all(grad_rows, "modes", split_axis=1, concat_axis=3, tiled=True)
        grad_spread = grad_spread.reshape(crop_count, 1, 2, band_count * slot_count, features)
        grad_narrow = jnp.einsum(
            "pjw,crpjd->crwd", forward_table, grad_spread, preferred_element_type=jnp.float32
        )
        grad_normed = (grad_middle + grad_narrow) * cell_mask
        grad_start = grad_middle + norm_backward(grad_normed, unit_one, factor_one, gain_one)
        input_grads.append((grad_start * cell_mask).astype(jnp.bfloat16))
        spectral_acc = spectral_acc + jnp.stack(
            [fold_complex(grad_mix_first), fold_complex(grad_mix_second)]
        )
        norm_rows_grad = jnp.stack(
            [
                jnp.sum(grad_normed * unit_one, axis=(0, 1, 2)),
                jnp.sum(grad_normed, axis=(0, 1, 2)),
                jnp.sum(grad_tokens * unit_two, axis=(0, 1, 2)),
                jnp.sum(grad_tokens, axis=(0, 1, 2)),
            ]
        )
        vector_acc = vector_acc + jnp.concatenate(
            [
                norm_rows_grad,
                jnp.sum(grad_first, axis=(0, 1, 3)),
                jnp.sum(grad_shrink, axis=(0, 1, 3)),
                jnp.sum(grad_flat, axis=0)[None, :],
                jnp.sum(grad_upper, axis=0).reshape(-1, features),
            ]
        )
    spectral_sum, vector_sum, dense_squares = lax.psum(
        (spectral_acc, vector_acc, jnp.sum(dense_grad * dense_grad)), ("dp", "modes")
    )
    squares = (
        dense_squares + jnp.sum(spectral_sum * spectral_sum) + jnp.sum(vector_sum * vector_sum)
    )
    grad_norm = jnp.sqrt(squares)
    clip_factor = jnp.minimum(1.0, CLIP_LEVEL / (grad_norm + 1e-06))
    dense_clipped = dense_grad * clip_factor
    spectral_clipped = spectral_sum * clip_factor
    vector_clipped = vector_sum * clip_factor
    dense_new, dense_first_new, dense_second_new = adam_update(
        dense_master, dense_first, dense_second, dense_clipped, RATE_MATRIX, DECAY_MATRIX
    )
    spectral_new, spectral_first_new, spectral_second_new = adam_update(
        spectral_master,
        spectral_first,
        spectral_second,
        spectral_clipped,
        RATE_MATRIX,
        DECAY_MATRIX,
    )
    vector_new, vector_first_new, vector_second_new = adam_update(
        vector_master, vector_first, vector_second, vector_clipped, RATE_VECTOR, 0.0
    )
    return (
        jnp.stack(outputs),
        jnp.stack(input_grads),
        grad_norm,
        dense_clipped,
        dense_new,
        dense_first_new,
        dense_second_new,
        spectral_clipped,
        spectral_new,
        spectral_first_new,
        spectral_second_new,
        vector_clipped,
        vector_new,
        vector_first_new,
        vector_second_new,
    )


def solution(mesh):
    return jax.shard_map(
        on_device,
        mesh=mesh,
        in_specs=(
            P(None, "dp", "modes", None, None),
            P(None, "dp", "modes", None, None),
            P(None, "dp"),
            P(None, "dp"),
            P(),
            P(("dp", "modes"), None, None),
            P(("dp", "modes"), None, None),
            P(("dp", "modes"), None, None),
            P(),
            P(),
            P(),
            P(),
            P(),
            P(),
        ),
        out_specs=(
            P(None, "dp", "modes", None, None),
            P(None, "dp", "modes", None, None),
            P(),
            P(("dp", "modes"), None, None),
            P(("dp", "modes"), None, None),
            P(("dp", "modes"), None, None),
            P(("dp", "modes"), None, None),
            P(),
            P(),
            P(),
            P(),
            P(),
            P(),
            P(),
            P(),
        ),
        check_vma=False,
    )
```

profile of v0, /device:TPU:0, one launch (start us, length us, event | category | flops | bytes accessed | tf_op | source)
XLA Modules:
  0.0 1283.3 jit_solution(5077845614989019208)
XLA Ops:
  21.1 5.8 multiply_convert_fusion.13
  30.9 6.3 all-to-all-start.6
  44.4 30.8 %all-to-all-done.6 = bf16[1,1,2,8,64,768]{5,2,4,1,0,3:T(2,128)(2,1)} async-done(((bf16[1,1,2,8,64,768]{5,2,4,1,0,3:T(2,128)(2,1)}), bf16[1,1,2,8,64,768]{5,2,4,1,0,3:T(2,128)(2,1)}, u32[]{:S(2)}, u32[]{:S(2)}) %all-to-all-start.6) | async-done | bytes 1572896 | tf_op jit(solution)/shard_map/all_to_all | solution.py:171
  86.9 30.6 %all-to-all-done.2 = bf16[1,1,2,8,64,768]{5,2,4,1,0,3:T(2,128)(2,1)} async-done(((bf16[1,1,2,8,64,768]{5,2,4,1,0,3:T(2,128)(2,1)}), bf16[1,1,2,8,64,768]{5,2,4,1,0,3:T(2,128)(2,1)}, u32[]{:S(2)}, u32[]{:S(2)}) %all-to-all-start.2) | async-done | bytes 1572896 | tf_op jit(solution)/shard_map/all_to_all | solution.py:171
  127.9 31.7 %all-to-all-done.4 = bf16[1,1,2,8,64,768]{5,2,4,1,0,3:T(2,128)(2,1)} async-done(((bf16[1,1,2,8,64,768]{5,2,4,1,0,3:T(2,128)(2,1)}), bf16[1,1,2,8,64,768]{5,2,4,1,0,3:T(2,128)(2,1)}, u32[]{:S(2)}, u32[]{:S(2)}) %all-to-all-start.4) | async-done | bytes 1572896 | tf_op jit(solution)/shard_map/all_to_all | solution.py:171
  184.8 23.2 %all-to-all-done = bf16[1,1,2,8,64,768]{5,2,4,1,0,3:T(2,128)(2,1)} async-done(((bf16[1,1,2,8,64,768]{5,2,4,1,0,3:T(2,128)(2,1)}), bf16[1,1,2,8,64,768]{5,2,4,1,0,3:T(2,128)(2,1)}, u32[]{:S(2)}, u32[]{:S(2)}) %all-to-all-start) | async-done | bytes 1572896 | tf_op jit(solution)/shard_map/all_to_all | solution.py:171
  225.7 7.2 fusion.110
  236.2 5.3 copy.673
  241.6 5.1 reshape.4017
  251.1 5.3 copy.660
  256.4 5.4 reshape.4009
  266.2 5.3 copy.647
  271.5 5.1 reshape.4001
  280.9 5.3 copy.633
  286.2 5.1 reshape.3993
  291.2 7.8 fusion.267
  311.0 32.9 %all-to-all-done.1 = bf16[1,8,2,1,64,768]{5,2,4,3,0,1:T(2,128)(2,1)S(1)} async-done(((bf16[1,8,2,1,64,768]{5,2,4,3,0,1:T(2,128)(2,1)}), bf16[1,8,2,1,64,768]{5,2,4,3,0,1:T(2,128)(2,1)S(1)}, u32[]{:S(2)}, u32[]{:S(2)}) %all-to-all-start.1) | async-done | bytes 1572896 | tf_op jit(solution)/shard_map/all_to_all | solution.py:188
  353.0 33.0 %all-to-all-done.3 = bf16[1,8,2,1,64,768]{5,2,4,3,0,1:T(2,128)(2,1)} async-done(((bf16[1,8,2,1,64,768]{5,2,4,3,0,1:T(2,128)(2,1)}), bf16[1,8,2,1,64,768]{5,2,4,3,0,1:T(2,128)(2,1)}, u32[]{:S(2)}, u32[]{:S(2)}) %all-to-all-start.3) | async-done | bytes 1572896 | tf_op jit(solution)/shard_map/all_to_all | solution.py:188
  395.2 33.0 %all-to-all-done.5 = bf16[1,8,2,1,64,768]{5,2,4,3,0,1:T(2,128)(2,1)} async-done(((bf16[1,8,2,1,64,768]{5,2,4,3,0,1:T(2,128)(2,1)}), bf16[1,8,2,1,64,768]{5,2,4,3,0,1:T(2,128)(2,1)}, u32[]{:S(2)}, u32[]{:S(2)}) %all-to-all-start.5) | async-done | bytes 1572896 | tf_op jit(solution)/shard_map/all_to_all | solution.py:188
  445.5 6.8 copy.1011
  465.6 5.3 reshape.4217
  470.9 5.1 reshape.4214
  476.0 5.1 reshape.4211
  481.0 5.1 reshape.4208
  502.3 5.5 fusion.420
  507.9 7.5 fusion.582
  515.4 5.6 convolution_bitcast_fusion.1
  527.4 5.4 fusion.421
  532.9 10.7 fusion.584
  549.9 5.9 fusion.422
  555.8 10.7 fusion.588
  574.1 5.9 fusion.423
  580.1 10.9 fusion.586
  598.4 5.3 fusion.292
  620.8 5.2 all-to-all-start.8
  631.8 5.8 convolution_bitcast_fusion.5
  637.6 5.6 convolution_bitcast_fusion.7
  643.2 6.9 convolution_bitcast_fusion
  650.2 6.9 convolution_bitcast_fusion.2
  657.1 6.8 all-to-all-done.8
  668.5 8.7 convolution_bitcast_fusion.3
  677.2 10.9 convolution_bitcast_fusion.4
  688.1 6.9 convolution_bitcast_fusion.6
  695.1 5.2 fusion.569
  700.3 6.0 all-to-all-done.12
  711.0 5.1 fusion.570
  725.9 8.0 fusion.31
  753.2 6.1 fusion.568
  770.2 7.6 fusion.43
  777.9 8.8 fusion.564
  791.0 6.1 fusion.571
  806.0 10.5 fusion.566
  837.0 31.8 %fusion.1 = f32[3072,2,768]{2,0,1:T(8,128)} fusion(f32[3072,1,768]{2,0,1:T(8,128)} %convolution_bitcast_fusion.6, f32[3072,1,768]{2,0,1:T(8,128)} %convolution_bitcast_fusion.7, f32[3072,1,768]{2,0,1:T(8,128)} %convolution_bitcast_fusion.4, f32[3072,1,768]{2,0,1:T(8,128)} %convolution_bitcast_fusion.5, f32[3072,1,768]{2,0,1:T(8,128)} %convolution_bitcast_fusion.2, ...), kind=kLoop, calls=%fused_computation.2 | loop fusion | flops 33030144 | bytes 94371840 | tf_op jit(solution)/shard_map/add | solution.py:220
  897.4 28.4 %all-to-all-done.13 = bf16[1,8,2,1,64,768]{5,2,4,3,0,1:T(2,128)(2,1)} async-done(((bf16[1,8,2,1,64,768]{5,2,4,3,0,1:T(2,128)(2,1)}), bf16[1,8,2,1,64,768]{5,2,4,3,0,1:T(2,128)(2,1)}, u32[]{:S(2)}, u32[]{:S(2)}) %all-to-all-start.13) | async-done | bytes 1572896 | tf_op jit(solution)/shard_map/all_to_all | solution.py:276
  941.6 8.5 fusion.412
  960.1 15.1 %all-to-all-done.9 = bf16[1,8,2,1,64,768]{5,2,4,3,0,1:T(2,128)(2,1)} async-done(((bf16[1,8,2,1,64,768]{5,2,4,3,0,1:T(2,128)(2,1)}), bf16[1,8,2,1,64,768]{5,2,4,3,0,1:T(2,128)(2,1)}, u32[]{:S(2)}, u32[]{:S(2)}) %all-to-all-start.9) | async-done | bytes 1572896 | tf_op jit(solution)/shard_map/all_to_all | solution.py:276
  979.6 8.5 fusion.411
  988.1 8.6 fusion.410
  1006.0 11.4 all-to-all-done.11
  1022.0 8.6 fusion.409
  1050.0 28.9 %all-to-all-done.15 = bf16[1,8,2,1,64,768]{5,2,4,3,0,1:T(2,128)(2,1)} async-done(((bf16[1,8,2,1,64,768]{5,2,4,3,0,1:T(2,128)(2,1)}), bf16[1,8,2,1,64,768]{5,2,4,3,0,1:T(2,128)(2,1)}, u32[]{:S(2)}, u32[]{:S(2)}) %all-to-all-start.15) | async-done | bytes 1572896 | tf_op jit(solution)/shard_map/all_to_all | solution.py:276
  1092.7 112.9 %reduce-scatter.2.cloned.1.call-done = f32[96,2,768]{2,0,1:T(8,128)} async-done(((f32[3072,2,768]{2,0,1:T(8,128)}), f32[96,2,768]{2,0,1:T(8,128)}) %reduce-scatter.2.cloned.1.call-update) | async-done | bytes 589840 | tf_op jit(solution)/shard_map/reduce_scatter | solution.py:220
  1210.2 39.9 %all-reduce = (f32[]{:T(128)}, f32[13,768]{1,0:T(8,128)S(1)}) all-reduce(f32[]{:T(128)} %multiply_reduce_fusion.13, f32[13,768]{1,0:T(8,128)S(1)} %add_add_fusion), channel_id=1, replica_groups=mesh['dp'=4,'modes'=8] {'dp','modes'}, use_global_device_ids=true, to_apply=%region_39.40 | all-reduce | flops 9985 | bytes 79880 | tf_op jit(solution)/shard_map/psum | solution.py:304
  1252.8 5.8 multiply_subtract_fusion
  (761 shorter events, 439.2 us)
Async XLA Ops:
  15.7 108.2 %copy-start.190 = (f32[768]{0:T(1024)}, f32[768]{0:T(1024)S(1)}, u32[]{:S(2)}) copy-start(f32[768]{0:T(1024)S(1)} %get-tuple-element.116) | copy-start | bytes 9220
  15.8 484.9 %copy-start.146 = (f32[768]{0:T(1024)}, f32[768]{0:T(1024)S(1)}, u32[]{:S(2)}) copy-start(f32[768]{0:T(1024)S(1)} %get-tuple-element.117) | copy-start | bytes 9220
  19.2 481.4 %copy-start.18 = (bf16[1,1,1,512,768]{3,4,2,1,0:T(8,128)(2,1)}, bf16[1,1,1,512,768]{3,4,2,1,0:T(8,128)(2,1)S(1)}, u32[]{:S(2)}) copy-start(bf16[1,1,1,512,768]{3,4,2,1,0:T(8,128)(2,1)S(1)} %copy.1053) | copy-start | bytes 2359300
  20.5 622.7 %copy-start.140 = (f32[512]{0:T(512)}, f32[512]{0:T(512)S(1)}, u32[]{:S(2)}) copy-start(f32[512]{0:T(512)S(1)} %fusion.548) | copy-start | bytes 6148
  20.8 479.8 %copy-start.152 = (f32[512]{0:T(512)}, f32[512]{0:T(512)S(1)}, u32[]{:S(2)}) copy-start(f32[512]{0:T(512)S(1)} %broadcast_multiply_fusion.20) | copy-start | bytes 6148
  26.9 97.0 %copy-start.120 = (bf16[1,512,512]{2,1,0:T(8,128)(2,1)}, bf16[1,512,512]{2,1,0:T(8,128)(2,1)S(1)}, u32[]{:S(2)}) copy-start(bf16[1,512,512]{2,1,0:T(8,128)(2,1)S(1)} %get-tuple-element.221) | copy-start | bytes 1572868
  26.9 97.0 %copy-start.122 = (bf16[1,512,512]{2,1,0:T(8,128)(2,1)}, bf16[1,512,512]{2,1,0:T(8,128)(2,1)S(1)}, u32[]{:S(2)}) copy-start(bf16[1,512,512]{2,1,0:T(8,128)(2,1)S(1)} %get-tuple-element.222) | copy-start | bytes 1572868
  30.9 44.3 %all-to-all-start.6 = ((bf16[1,1,2,8,64,768]{5,2,4,1,0,3:T(2,128)(2,1)}), bf16[1,1,2,8,64,768]{5,2,4,1,0,3:T(2,128)(2,1)}, u32[]{:S(2)}, u32[]{:S(2)}) async-start(bf16[1,1,2,8,64,768]{5,2,4,1,0,3:T(2,128)(2,1)} %copy.668), calls=%async_computation.6 | async-start | bytes 3145728 | tf_op jit(solution)/shard_map/all_to_all | solution.py:171
  39.9 637.3 %copy-start.144 = (f32[512]{0:T(512)}, f32[512]{0:T(512)S(1)}, u32[]{:S(2)}) copy-start(f32[512]{0:T(512)S(1)} %fusion.544) | copy-start | bytes 6148
  75.1 42.3 %all-to-all-start.2 = ((bf16[1,1,2,8,64,768]{5,2,4,1,0,3:T(2,128)(2,1)}), bf16[1,1,2,8,64,768]{5,2,4,1,0,3:T(2,128)(2,1)}, u32[]{:S(2)}, u32[]{:S(2)}) async-start(bf16[1,1,2,8,64,768]{5,2,4,1,0,3:T(2,128)(2,1)} %copy.642), calls=%async_computation.2 | async-start | bytes 3145728 | tf_op jit(solution)/shard_map/all_to_all | solution.py:171
  82.4 567.8 %copy-start.142 = (f32[512]{0:T(512)}, f32[512]{0:T(512)S(1)}, u32[]{:S(2)}) copy-start(f32[512]{0:T(512)S(1)} %fusion.546) | copy-start | bytes 6148
  82.6 416.2 %copy-start.156 = (f32[512]{0:T(512)}, f32[512]{0:T(512)S(1)}, u32[]{:S(2)}) copy-start(f32[512]{0:T(512)S(1)} %broadcast_multiply_fusion.22) | copy-start | bytes 6148
  117.5 42.1 %all-to-all-start.4 = ((bf16[1,1,2,8,64,768]{5,2,4,1,0,3:T(2,128)(2,1)}), bf16[1,1,2,8,64,768]{5,2,4,1,0,3:T(2,128)(2,1)}, u32[]{:S(2)}, u32[]{:S(2)}) async-start(bf16[1,1,2,8,64,768]{5,2,4,1,0,3:T(2,128)(2,1)} %copy.655), calls=%async_computation.4 | async-start | bytes 3145728 | tf_op jit(solution)/shard_map/all_to_all | solution.py:171
  127.9 36.3 %copy-start.95 = (f32[96,2,768]{2,1,0:T(2,128)S(1)}, f32[96,2,768]{2,1,0:T(2,128)}, u32[]{:S(2)}) copy-start(f32[96,2,768]{2,1,0:T(2,128)} %param.19) | copy-start | bytes 1769476
  127.9 37.1 %copy-start.198 = (pred[64]{0:T(512)(128)(4,1)S(1)}, pred[64]{0:T(512)(128)(4,1)}, u32[]{:S(2)}) copy-start(pred[64]{0:T(512)(128)(4,1)} %get-tuple-element.233) | copy-start | bytes 196
  127.9 37.1 %copy-start.134 = (f32[13,768]{1,0:T(8,128)S(1)}, f32[13,768]{1,0:T(8,128)}, u32[]{:S(2)}) copy-start(f32[13,768]{1,0:T(8,128)} %param.25) | copy-start | bytes 119812
  127.9 37.2 %copy-start.78 = (f32[2,2,8,96,96]{4,3,2,1,0:T(8,128)S(1)}, f32[2,2,8,96,96]{4,3,2,1,0:T(8,128)}, u32[]{:S(2)}) copy-start(f32[2,2,8,96,96]{4,3,2,1,0:T(8,128)} %param.22) | copy-start | bytes 3538948
  159.6 48.4 %all-to-all-start = ((bf16[1,1,2,8,64,768]{5,2,4,1,0,3:T(2,128)(2,1)}), bf16[1,1,2,8,64,768]{5,2,4,1,0,3:T(2,128)(2,1)}, u32[]{:S(2)}, u32[]{:S(2)}) async-start(bf16[1,1,2,8,64,768]{5,2,4,1,0,3:T(2,128)(2,1)} %copy.627), calls=%async_computation | async-start | bytes 3145728 | tf_op jit(solution)/shard_map/all_to_all | solution.py:171
  163.9 338.3 %all-gather.2.cloned.1.call-start = ((), (), s32[]{:S(2)}) async-start(), calls=%async_computation.17 | async-start | bytes 9732096 | tf_op jit(solution)/shard_map/all_gather | solution.py:93
  165.0 126.2 %copy-start.196 = (f32[64]{0:T(128)}, f32[64]{0:T(128)S(1)}, u32[]{:S(2)}) copy-start(f32[64]{0:T(128)S(1)} %convert_element_type.952) | copy-start | bytes 772
  165.1 126.2 %copy-start.154 = (f32[2,768]{1,0:T(2,128)}, f32[2,768]{1,0:T(2,128)S(1)}, u32[]{:S(2)}) copy-start(f32[2,768]{1,0:T(2,128)S(1)} %get-tuple-element.185) | copy-start | bytes 18436
  165.2 60.3 %copy-start.150 = (f32[2,8,96]{2,0,1:T(2,128)}, f32[2,8,96]{2,0,1:T(2,128)S(1)}, u32[]{:S(2)}) copy-start(f32[2,8,96]{2,0,1:T(2,128)S(1)} %copy.630) | copy-start | bytes 18436
  165.5 42.6 %copy-start.130 = (bf16[1,8,2,8]{3,1,2,0:T(8,128)(2,1)}, bf16[1,8,2,8]{3,1,2,0:T(8,128)(2,1)S(1)}, u32[]{:S(2)}) copy-start(bf16[1,8,2,8]{3,1,2,0:T(8,128)(2,1)S(1)} %get-tuple-element.216) | copy-start | bytes 772
  165.5 42.6 %copy-start.132 = (bf16[1,8,2,8]{3,1,2,0:T(8,128)(2,1)}, bf16[1,8,2,8]{3,1,2,0:T(8,128)(2,1)S(1)}, u32[]{:S(2)}) copy-start(bf16[1,8,2,8]{3,1,2,0:T(8,128)(2,1)S(1)} %get-tuple-element.223) | copy-start | bytes 772
  165.5 224.8 %copy-start.136 = (bf16[1,8,2,8]{3,1,2,0:T(8,128)(2,1)}, bf16[1,8,2,8]{3,1,2,0:T(8,128)(2,1)S(1)}, u32[]{:S(2)}) copy-start(bf16[1,8,2,8]{3,1,2,0:T(8,128)(2,1)S(1)} %get-tuple-element.215) | copy-start | bytes 772
  165.5 224.8 %copy-start.138 = (bf16[1,8,2,8]{3,1,2,0:T(8,128)(2,1)}, bf16[1,8,2,8]{3,1,2,0:T(8,128)(2,1)S(1)}, u32[]{:S(2)}) copy-start(bf16[1,8,2,8]{3,1,2,0:T(8,128)(2,1)S(1)} %get-tuple-element.224) | copy-start | bytes 772
  167.6 56.1 %copy-start.50 = (bf16[1,2,8,96,96]{4,3,0,1,2:T(8,128)(2,1)}, bf16[1,2,8,96,96]{4,3,0,1,2:T(8,128)(2,1)S(1)}, u32[]{:S(2)}) copy-start(bf16[1,2,8,96,96]{4,3,0,1,2:T(8,128)(2,1)S(1)} %get-tuple-element.183) | copy-start | bytes 884740
  302.5 41.3 %all-to-all-start.1 = ((bf16[1,8,2,1,64,768]{5,2,4,3,0,1:T(2,128)(2,1)}), bf16[1,8,2,1,64,768]{5,2,4,3,0,1:T(2,128)(2,1)S(1)}, u32[]{:S(2)}, u32[]{:S(2)}) async-start(bf16[1,8,2,1,64,768]{5,2,4,3,0,1:T(2,128)(2,1)} %copy.635), calls=%async_computation.1 | async-start | bytes 3145728 | tf_op jit(solution)/shard_map/all_to_all | solution.py:188
  343.9 42.1 %all-to-all-start.3 = ((bf16[1,8,2,1,64,768]{5,2,4,3,0,1:T(2,128)(2,1)}), bf16[1,8,2,1,64,768]{5,2,4,3,0,1:T(2,128)(2,1)}, u32[]{:S(2)}, u32[]{:S(2)}) async-start(bf16[1,8,2,1,64,768]{5,2,4,3,0,1:T(2,128)(2,1)} %copy.649), calls=%async_computation.3 | async-start | bytes 3145728 | tf_op jit(solution)/shard_map/all_to_all | solution.py:188
  386.0 42.1 %all-to-all-start.5 = ((bf16[1,8,2,1,64,768]{5,2,4,3,0,1:T(2,128)(2,1)}), bf16[1,8,2,1,64,768]{5,2,4,3,0,1:T(2,128)(2,1)}, u32[]{:S(2)}, u32[]{:S(2)}) async-start(bf16[1,8,2,1,64,768]{5,2,4,3,0,1:T(2,128)(2,1)} %copy.662), calls=%async_computation.5 | async-start | bytes 3145728 | tf_op jit(solution)/shard_map/all_to_all | solution.py:188
  428.1 65.1 %all-to-all-start.7 = ((bf16[1,8,2,1,64,768]{5,2,4,3,0,1:T(2,128)(2,1)}), bf16[1,8,2,1,64,768]{5,2,4,3,0,1:T(2,128)(2,1)}, u32[]{:S(2)}, u32[]{:S(2)}) async-start(bf16[1,8,2,1,64,768]{5,2,4,3,0,1:T(2,128)(2,1)} %copy.675), calls=%async_computation.7 | async-start | bytes 3145728 | tf_op jit(solution)/shard_map/all_to_all | solution.py:188
  501.9 13.5 %copy-start.20 = (f32[1,1,512,768]{2,3,1,0:T(8,128)}, f32[1,1,512,768]{2,3,1,0:T(8,128)S(1)}, u32[]{:S(2)}) copy-start(f32[1,1,512,768]{2,3,1,0:T(8,128)S(1)} %get-tuple-element.236) | copy-start | bytes 4718596
  527.4 16.2 %slice-start = ((s8[9437184]{0:T(1024)(128)(4,1)}), s8[4194304]{0:T(1024)(128)(4,1)S(1)}, s32[]{:S(2)}) async-start(s8[9437184]{0:T(1024)(128)(4,1)} %bitcast.1690), calls=%async_computation.20 | async-start | bytes 8388608
  532.9 10.7 copy-start.211
  532.9 10.7 slice-start.1
  532.9 10.7 slice-start.2
  549.9 16.7 %slice-start.3 = ((s8[9437184]{0:T(1024)(128)(4,1)}), s8[4194304]{0:T(1024)(128)(4,1)S(1)}, s32[]{:S(2)}) async-start(s8[9437184]{0:T(1024)(128)(4,1)} %bitcast.1692), calls=%async_computation.23 | async-start | bytes 8388608
  555.8 10.7 copy-start.212
  555.8 10.7 slice-start.4
  555.8 10.7 slice-start.5
  574.1 16.9 %slice-start.6 = ((s8[9437184]{0:T(1024)(128)(4,1)}), s8[4194304]{0:T(1024)(128)(4,1)S(1)}, s32[]{:S(2)}) async-start(s8[9437184]{0:T(1024)(128)(4,1)} %bitcast.1694), calls=%async_computation.26 | async-start | bytes 8388608
  580.0 10.9 copy-start.210
  580.0 10.9 slice-start.7
  580.0 10.9 slice-start.8
  607.4 9.4 copy-start.75
  620.8 43.1 %all-to-all-start.8 = ((bf16[1,1,2,8,64,768]{5,2,4,1,0,3:T(2,128)(2,1)}), bf16[1,1,2,8,64,768]{5,2,4,1,0,3:T(2,128)(2,1)}, u32[]{:S(2)}, u32[]{:S(2)}) async-start(bf16[1,1,2,8,64,768]{5,2,4,1,0,3:T(2,128)(2,1)} %copy.682), calls=%async_computation.8 | async-start | bytes 3145728 | tf_op jit(solution)/shard_map/all_to_all | solution.py:233
  631.8 11.4 slice-start.13
  637.6 12.6 slice-start.11
  663.9 42.3 %all-to-all-start.12 = ((bf16[1,1,2,8,64,768]{5,2,4,1,0,3:T(2,128)(2,1)}), bf16[1,1,2,8,64,768]{5,2,4,1,0,3:T(2,128)(2,1)}, u32[]{:S(2)}, u32[]{:S(2)}) async-start(bf16[1,1,2,8,64,768]{5,2,4,1,0,3:T(2,128)(2,1)} %copy.718), calls=%async_computation.12 | async-start | bytes 3145728 | tf_op jit(solution)/shard_map/all_to_all | solution.py:233
  668.5 19.6 %slice-start.9 = ((s8[6291456]{0:T(1024)(128)(4,1)}), s8[4194304]{0:T(1024)(128)(4,1)S(1)}, s32[]{:S(2)}) async-start(s8[6291456]{0:T(1024)(128)(4,1)} %bitcast.1696), calls=%async_computation.29 | async-start | bytes 8388608
  677.2 10.9 copy-start.69
  677.2 10.9 slice-start.10
  700.3 10.7 copy-start.92
  706.3 42.5 %all-to-all-start.10 = ((bf16[1,1,2,8,64,768]{5,2,4,1,0,3:T(2,128)(2,1)}), bf16[1,1,2,8,64,768]{5,2,4,1,0,3:T(2,128)(2,1)}, u32[]{:S(2)}, u32[]{:S(2)}) async-start(bf16[1,1,2,8,64,768]{5,2,4,1,0,3:T(2,128)(2,1)} %copy.700), calls=%async_computation.10 | async-start | bytes 3145728 | tf_op jit(solution)/shard_map/all_to_all | solution.py:233
  748.8 42.1 %all-to-all-start.14 = ((bf16[1,1,2,8,64,768]{5,2,4,1,0,3:T(2,128)(2,1)}), bf16[1,1,2,8,64,768]{5,2,4,1,0,3:T(2,128)(2,1)}, u32[]{:S(2)}, u32[]{:S(2)}) async-start(bf16[1,1,2,8,64,768]{5,2,4,1,0,3:T(2,128)(2,1)} %copy.736), calls=%async_computation.14 | async-start | bytes 3145728 | tf_op jit(solution)/shard_map/all_to_all | solution.py:233
  753.1 281.2 %all-reduce.3.cloned.1.call-start = ((), (), s32[]{:S(2)}) async-start(), calls=%async_computation.18 | async-start | bytes 3145728 | tf_op jit(solution)/shard_map/psum | solution.py:304
  837.0 368.6 %reduce-scatter.2.cloned.1.call-start = ((), (), s32[]{:S(2)}) async-start(), calls=%async_computation.19 | async-start | bytes 19464192 | tf_op jit(solution)/shard_map/reduce_scatter | solution.py:220
  881.6 44.2 %all-to-all-start.13 = ((bf16[1,8,2,1,64,768]{5,2,4,3,0,1:T(2,128)(2,1)}), bf16[1,8,2,1,64,768]{5,2,4,3,0,1:T(2,128)(2,1)}, u32[]{:S(2)}, u32[]{:S(2)}) async-start(bf16[1,8,2,1,64,768]{5,2,4,3,0,1:T(2,128)(2,1)} %copy.730), calls=%async_computation.13 | async-start | bytes 3145728 | tf_op jit(solution)/shard_map/all_to_all | solution.py:276
  897.4 33.1 %copy-start.79 = (f32[2,2,8,96,96]{4,3,2,1,0:T(8,128)S(1)}, f32[2,2,8,96,96]{4,3,2,1,0:T(8,128)}, u32[]{:S(2)}) copy-start(f32[2,2,8,96,96]{4,3,2,1,0:T(8,128)} %param.22) | copy-start | bytes 3538948
  925.7 49.4 %all-to-all-start.9 = ((bf16[1,8,2,1,64,768]{5,2,4,3,0,1:T(2,128)(2,1)}), bf16[1,8,2,1,64,768]{5,2,4,3,0,1:T(2,128)(2,1)}, u32[]{:S(2)}, u32[]{:S(2)}) async-start(bf16[1,8,2,1,64,768]{5,2,4,3,0,1:T(2,128)(2,1)} %copy.694), calls=%async_computation.9 | async-start | bytes 3145728 | tf_op jit(solution)/shard_map/all_to_all | solution.py:276
  960.1 19.5 %copy-start.34 = (f32[1,1,512,768]{2,3,1,0:T(8,128)S(1)}, f32[1,1,512,768]{2,3,1,0:T(8,128)}, u32[]{:S(2)}) copy-start(f32[1,1,512,768]{2,3,1,0:T(8,128)} %copy-done.31) | copy-start | bytes 4718596
  975.1 42.3 %all-to-all-start.11 = ((bf16[1,8,2,1,64,768]{5,2,4,3,0,1:T(2,128)(2,1)}), bf16[1,8,2,1,64,768]{5,2,4,3,0,1:T(2,128)(2,1)}, u32[]{:S(2)}, u32[]{:S(2)}) async-start(bf16[1,8,2,1,64,768]{5,2,4,3,0,1:T(2,128)(2,1)} %copy.712), calls=%async_computation.11 | async-start | bytes 3145728 | tf_op jit(solution)/shard_map/all_to_all | solution.py:276
  1006.0 16.0 %copy-start.26 = (f32[1,1,512,768]{2,3,1,0:T(8,128)S(1)}, f32[1,1,512,768]{2,3,1,0:T(8,128)}, u32[]{:S(2)}) copy-start(f32[1,1,512,768]{2,3,1,0:T(8,128)} %copy-done.23) | copy-start | bytes 4718596
  1017.4 61.5 %all-to-all-start.15 = ((bf16[1,8,2,1,64,768]{5,2,4,3,0,1:T(2,128)(2,1)}), bf16[1,8,2,1,64,768]{5,2,4,3,0,1:T(2,128)(2,1)}, u32[]{:S(2)}, u32[]{:S(2)}) async-start(bf16[1,8,2,1,64,768]{5,2,4,3,0,1:T(2,128)(2,1)} %copy.748), calls=%async_computation.15 | async-start | bytes 3145728 | tf_op jit(solution)/shard_map/all_to_all | solution.py:276
  (184 other events, 654.1 us)
Sparse Core Ops, SparseCore 0:
  167.9 93.1 all-gather.1
  837.1 146.5 all-reduce.2
  990.1 215.4 reduce-scatter.1
where the time goes:
time: 1290 us; the launch traced here: 1280 us
  waiting for transfers between devices  432 us (33%)
  matrix products  323 us (25%)
  local copies, waits for them, and re-layouts  284 us (22%)
  other arithmetic  108 us (8%)
  starting transfers between devices  73.1 us (6%)
  blocking collectives  39.9 us (3%)
  between operations  23.7 us (2%)
    all_to_all x4, waiting for transfers between devices, on_device(): lax.all_to_all(to_owner, 'modes', split_axis=3, concat_axis=1, tiled=True)  116 us
    reduce_scatter x1, waiting for transfers between devices, on_device(): lax.psum_scatter(jnp.stack([up_grad, down_grad], axis=1), ('dp', 'modes')...  113 us
    all_to_all x4, waiting for transfers between devices, on_device(): lax.all_to_all(back_rows, 'modes', split_axis=1, concat_axis=3, tiled=True)  98.9 us
    all_to_all x4, waiting for transfers between devices, on_device(): lax.all_to_all(grad_rows, 'modes', split_axis=1, concat_axis=3, tiled=True)  83.8 us
    unnamed x480, local copies, waits for them, and re-layouts  68.1 us
    reshape x12, local copies, waits for them, and re-layouts, block_mix(): return mixed.reshape(values.shape)  61.4 us
    psum x1, blocking collectives, on_device(): lax.psum((spectral_acc, vector_acc, jnp.sum(dense_grad * dense_grad)), ('...  39.9 us
    dot_general x4, matrix products, on_device(): jnp.einsum('td,fd->tf', grad_low, weight_down, preferred_element_type=jnp...  39.8 us
  transfers between devices with their start and end apart: 19, of which 16 were waited for; matrix products, arithmetic and copies ran while one was open for 38% of the time, Pallas kernels for 0%

commit v1 on v0

v1 whole, which is shorter than its diff:
```python
import functools
import math

import jax
import jax.numpy as jnp
import ml_dtypes
import numpy as np
from jax import lax
from jax.experimental import pallas as pl
from jax.experimental.pallas import tpu as pltpu
from jax.sharding import PartitionSpec as P

NB = 8
BS = 96
STEP = 10

SHRINK_LEVEL = 0.01
NORM_EPS = 1e-05
CLIP_LEVEL = 1.0
BETA_FIRST = 0.9
BETA_SECOND = 0.95
ADAM_EPS = 1e-08
RATE_MATRIX = 0.05
RATE_VECTOR = 0.5
DECAY_MATRIX = 0.1

GELU_SCALE = math.sqrt(2.0 / math.pi)
GELU_CUBE = 0.044715
SPAN = 384
LANES = 128
VMEM = 63 * 2**20
SMALL = 24 * 2**20
F32 = jnp.float32
BF16 = jnp.bfloat16


def wave_tables(band_count, row_cells):
    wave_count = row_cells // 2
    slots = wave_count // band_count
    scale = (band_count * row_cells) ** (-0.5)
    waves = np.arange(wave_count)
    phase = (waves[:, None] * np.arange(row_cells)[None, :]) % row_cells
    angle = phase * (2.0 * math.pi / row_cells)
    factor = np.where(waves == 0, scale, 2.0 * scale)[:, None]

    def order(parts):
        parts = np.stack(parts).astype(np.float32).astype(ml_dtypes.bfloat16)
        parts = parts.reshape(2, band_count, slots, row_cells).transpose(1, 0, 2, 3)
        return np.ascontiguousarray(parts.reshape(2 * wave_count, row_cells))

    forward = order([np.cos(angle) * scale, -np.sin(angle) * scale])
    inverse = order([np.cos(angle) * factor, -np.sin(angle) * factor])
    return (
        jnp.asarray(forward),
        jnp.asarray(np.ascontiguousarray(forward.T)),
        jnp.asarray(inverse),
        jnp.asarray(np.ascontiguousarray(inverse.T)),
    )


def row_tables(length):
    row_index = jnp.arange(length, dtype=jnp.int32)
    phase_int = row_index[:, None] * row_index[None, :] % length
    angles = phase_int.astype(F32) * (2.0 * math.pi / length)
    cosine = jnp.cos(angles)
    sines = jnp.sin(angles)
    forward = jnp.stack([jnp.stack([cosine, sines], axis=1), jnp.stack([-sines, cosine], axis=1)])
    inverse = jnp.stack([jnp.stack([cosine, -sines], axis=1), jnp.stack([sines, cosine], axis=1)])
    return (forward.astype(BF16), inverse.astype(BF16))


def norm_forward(values):
    centered = values - jnp.mean(values, axis=-1, keepdims=True)
    factor = lax.rsqrt(jnp.mean(centered * centered, axis=-1, keepdims=True) + NORM_EPS)
    return (centered * factor, factor)


def norm_backward(grad_rows, unit_rows, factor, gain_row):
    scaled = grad_rows * gain_row
    return factor * (
        scaled
        - jnp.mean(scaled, axis=-1, keepdims=True)
        - unit_rows * jnp.mean(scaled * unit_rows, axis=-1, keepdims=True)
    )


def gelu_pair(values):
    square = values * values
    bend = jnp.tanh(values * (GELU_SCALE + (GELU_SCALE * GELU_CUBE) * square))
    half = 0.5 + 0.5 * bend
    slope = GELU_SCALE + (3.0 * GELU_SCALE * GELU_CUBE) * square
    return (values * half, half + (0.5 * values) * (1.0 - bend * bend) * slope)


def gelu_only(values):
    square = values * values
    bend = jnp.tanh(values * (GELU_SCALE + (GELU_SCALE * GELU_CUBE) * square))
    return values * (0.5 + 0.5 * bend)


def dot(left, right):
    return lax.dot_general(left, right, (((1,), (0,)), ((), ())), preferred_element_type=F32)


def dot_nt(left, right):
    return lax.dot_general(left, right, (((1,), (1,)), ((), ())), preferred_element_type=F32)


def dot_tn(left, right):
    return lax.dot_general(left, right, (((0,), (0,)), ((), ())), preferred_element_type=F32)


def adam_update(master, first_old, second_old, gradient, rate, decay):
    first_new = BETA_FIRST * first_old + (1.0 - BETA_FIRST) * gradient
    second_new = BETA_SECOND * second_old + (1.0 - BETA_SECOND) * gradient * gradient
    moved = (
        first_new
        / (1.0 - BETA_FIRST**STEP)
        / (jnp.sqrt(second_new / (1.0 - BETA_SECOND**STEP)) + ADAM_EPS)
    )
    return (master - rate * (moved + decay * master), first_new, second_new)


def valid_rows(count, rows):
    return lax.broadcasted_iota(jnp.int32, (rows, 1), 0) < count


def only(mask, values):
    return jnp.where(mask, values, 0.0)


def params(limit=VMEM):
    return pltpu.CompilerParams(vmem_limit_bytes=limit)


def cost(flops, moved, transcendentals=0):
    return pl.CostEstimate(
        flops=int(flops), bytes_accessed=int(moved), transcendentals=int(transcendentals)
    )


SMEM = pl.BlockSpec(memory_space=pltpu.SMEM)
ANY = pl.BlockSpec(memory_space=pl.ANY)
HBM = pl.BlockSpec(memory_space=pltpu.HBM)
VMEMS = pl.BlockSpec(memory_space=pltpu.VMEM)


def whole(array):
    zeros = (0,) * len(array.shape)
    return pl.BlockSpec(array.shape, lambda *_: zeros)


def tie(values, *ahead):
    return pl.pallas_call(
        lambda *_: None,
        in_specs=[HBM] * (1 + len(ahead)),
        out_specs=HBM,
        out_shape=jax.ShapeDtypeStruct(values.shape, values.dtype),
        input_output_aliases={0: 0},
        compiler_params=params(),
        name="tie",
    )(values, *ahead)


def swap(values, axis, mask):
    count = lax.axis_size(axis)
    return lax.ppermute(values, axis, [(i, i ^ mask) for i in range(count)])


def pick_call(kernel, shapes, *operands, name):
    return pl.pallas_call(
        kernel,
        out_shape=shapes,
        compiler_params=params(),
        cost_estimate=cost(0, 4 * sum(o.size for o in operands)),
        name=name,
    )(*operands)


def chunks_by_mask(values, count, index_of):
    shape = jax.ShapeDtypeStruct(values[0].shape[1:], values[0].dtype)

    def kernel(*refs):
        index = index_of()
        for s, out in enumerate(refs[len(values) :]):
            total = refs[0][pl.ds(index ^ s, 1)]
            for ref in refs[1 : len(values)]:
                total = total + ref[pl.ds(index ^ s, 1)]
            out[...] = total[0]

    return list(pick_call(kernel, [shape] * count, *values, name="sum_and_cut"))


def place_by_mask(parts, index_of):
    shape = jax.ShapeDtypeStruct((len(parts),) + parts[0].shape, parts[0].dtype)

    def kernel(*refs):
        index = index_of()
        for s, ref in enumerate(refs[:-1]):
            refs[-1][pl.ds(index ^ s, 1)] = ref[...][None]

    return pick_call(kernel, shape, *parts, name="place_blocks")


def dp_index():
    return lax.axis_index("dp")


def z_index():
    return lax.axis_index("modes") // 2


def scatter_spectral(keep, send):
    parts = chunks_by_mask([keep, swap(send, "modes", 1)], 4, dp_index)
    parts = parts[:1] + [swap(parts[s], "dp", s) for s in range(1, 4)]
    return chunks_by_mask(parts, 4, z_index)


def own_spectral(parts):
    own = parts[0] + swap(parts[1], "modes", 2)
    return own + (swap(parts[2], "modes", 4) + swap(parts[3], "modes", 6))


def gather_spectral(own, ahead):
    blocks = place_by_mask([tie(own, ahead)] + [swap(own, "modes", 2 * s) for s in range(1, 4)], z_index)
    blocks = place_by_mask([blocks] + [swap(blocks, "dp", s) for s in range(1, 4)], dp_index)
    return (blocks, swap(blocks, "modes", 1))


def sum_four(values, axis, stride):
    one, two, three = (swap(values, axis, s * stride) for s in (1, 2, 3))
    return (values + one) + (two + three)


def row_transform(real, imag, sign):
    diagonal = float(ml_dtypes.bfloat16(math.cos(math.pi / 4)))

    def turn(re, im):
        return (-im, re) if sign > 0 else (im, -re)

    def four(index):
        re = [real[i] for i in index]
        im = [imag[i] for i in index]
        sum_even = (re[0] + re[2], im[0] + im[2])
        gap_even = (re[0] - re[2], im[0] - im[2])
        sum_odd = (re[1] + re[3], im[1] + im[3])
        gap_odd = turn(re[1] - re[3], im[1] - im[3])
        return [
            (sum_even[0] + sum_odd[0], sum_even[1] + sum_odd[1]),
            (gap_even[0] + gap_odd[0], gap_even[1] + gap_odd[1]),
            (sum_even[0] - sum_odd[0], sum_even[1] - sum_odd[1]),
            (gap_even[0] - gap_odd[0], gap_even[1] - gap_odd[1]),
        ]

    even = four((0, 2, 4, 6))
    odd = four((1, 3, 5, 7))
    re, im = odd[1]
    side = turn(re, im)
    odd[1] = (diagonal * (re + side[0]), diagonal * (im + side[1]))
    odd[2] = turn(*odd[2])
    re, im = odd[3]
    side = turn(re, im)
    odd[3] = (diagonal * (side[0] - re), diagonal * (side[1] - im))
    out = [(e[0] + o[0], e[1] + o[1]) for e, o in zip(even, odd)]
    out += [(e[0] - o[0], e[1] - o[1]) for e, o in zip(even, odd)]
    return ([v[0] for v in out], [v[1] for v in out])


def tiles(slots, features):
    for row in range(0, slots, 16):
        for lane in range(0, features, LANES):
            yield row, lane, lane // SPAN, lane % SPAN


def rows_to_modes(rows_ref, modes_ref, first, slots, features):
    for row, lane, group, inner in tiles(slots, features):
        parts = [
            [
                rows_ref[h, p * slots + row : p * slots + row + 16, lane : lane + LANES].astype(F32)
                for h in range(8)
            ]
            for p in range(2)
        ]
        done = row_transform(parts[0], parts[1], -1)
        for p in range(2):
            for j in range(8):
                at = first + j * slots + row
                modes_ref[
                    group, at : at + 16, p * SPAN + inner : p * SPAN + inner + LANES
                ] = done[p][j].astype(modes_ref.dtype)


def modes_to_rows(modes_ref, rows_ref, first, slots, features):
    for row, lane, group, inner in tiles(slots, features):
        parts = [
            [
                modes_ref[
                    group,
                    first + j * slots + row : first + j * slots + row + 16,
                    p * SPAN + inner : p * SPAN + inner + LANES,
                ].astype(F32)
                for j in range(8)
            ]
            for p in range(2)
        ]
        done = row_transform(parts[0], parts[1], 1)
        for p in range(2):
            for h in range(8):
                rows_ref[
                    h, p * slots + row : p * slots + row + 16, lane : lane + LANES
                ] = done[p][h].astype(rows_ref.dtype)


def spread_kernel(first, heights, widths, patches, table, vectors, out, base):
    micro = first + pl.program_id(0)
    count = jnp.where(lax.axis_index("modes") < heights[micro], widths[micro], 0)
    mask = valid_rows(count, patches.shape[0])
    masked_in = only(mask, patches[...].astype(F32))
    unit, _ = norm_forward(masked_in)
    normed = only(mask, unit * vectors[0:1, :] + vectors[1:2, :])
    base[...] = masked_in + normed
    out[...] = dot(table[...], normed.astype(BF16)).astype(BF16).reshape(out.shape)


def mix_kernel(spectral, out):
    blocks = SPAN // BS
    row = lax.broadcasted_iota(jnp.int32, (BS, SPAN), 0)
    column = lax.broadcasted_iota(jnp.int32, (BS, SPAN), 1)
    for group in range(NB // blocks):
        for n in range(blocks):
            place = (column == row + n * BS).astype(F32).astype(BF16)
            re = dot(spectral[0, group * blocks + n].astype(BF16), place)
            im = dot(spectral[1, group * blocks + n].astype(BF16), place)
            top, low = n * BS, SPAN + n * BS
            out[group, top : top + BS, 0:SPAN] = re.astype(BF16)
            out[group, top : top + BS, SPAN:] = im.astype(BF16)
            out[group, low : low + BS, 0:SPAN] = (-im).astype(BF16)
            out[group, low : low + BS, SPAN:] = re.astype(BF16)


def keep_column(limits, slots, rows, micros):
    wave = limits[micros] + lax.broadcasted_iota(jnp.int32, (rows, 1), 0) % slots
    return (wave < limits[micros + 1]).astype(F32)


def filter_kernel(slots, micros, limits, received, mix, bias, modes, back, shrunk):
    features = received.shape[-1]
    crops, size = received.shape[1], 8 * slots
    keep = keep_column(limits, slots, modes.shape[1], micros)
    for crop in range(crops):
        rows_to_modes(received.at[:, crop], modes, crop * size, slots, features)
    for group in range(features // SPAN):
        pre_active = dot(modes[group], mix[0, group]) + bias[0, group]
        active = gelu_only(pre_active).astype(BF16)
        pre_shrink = dot(active, mix[1, group]) + bias[1, group]
        value = pre_shrink - SHRINK_LEVEL * jnp.tanh(pre_shrink * (1.0 / SHRINK_LEVEL))
        shrunk[group] = (keep * value).astype(BF16)
    for crop in range(crops):
        modes_to_rows(shrunk, back.at[:, crop], crop * size, slots, features)


def filter_back_kernel(slots, micros, limits, received, modes, mix, bias, *rest):
    spread, sums, mine, other, full, turned = rest[-6:]
    before = rest[:-6]
    features = received.shape[-1]
    crops, size = received.shape[1], 8 * slots
    keep = keep_column(limits, slots, modes.shape[1], micros)
    for crop in range(crops):
        rows_to_modes(received.at[:, crop], turned, crop * size, slots, features)
    for group in range(features // SPAN):
        pre_active = dot(modes[group], mix[0, group]) + bias[0, group]
        value, slope = gelu_pair(pre_active)
        active = value.astype(BF16)
        pre_shrink = dot(active, mix[1, group]) + bias[1, group]
        bend = jnp.tanh(pre_shrink * (1.0 / SHRINK_LEVEL))
        grad_shrink = turned[group] * (keep * bend * bend)
        shrink_low = grad_shrink.astype(BF16)
        grad_first = dot_nt(shrink_low, mix[1, group]) * slope
        first_low = grad_first.astype(BF16)
        sums[group, 0:1, :] = jnp.sum(grad_first, axis=0, keepdims=True)
        sums[group, 1:2, :] = jnp.sum(grad_shrink, axis=0, keepdims=True)
        full[0, group] = dot_tn(modes[group], first_low)
        full[1, group] = dot_tn(active, shrink_low)
        turned[group] = dot_nt(first_low, mix[0, group]).astype(BF16).astype(F32)
    for crop in range(crops):
        modes_to_rows(turned, spread.at[:, crop], crop * size, slots, features)

    blocks = SPAN // BS
    for layer in range(2):
        for group in range(features // SPAN):
            for n in range(blocks):
                top = slice(n * BS, n * BS + BS)
                low = slice(SPAN + n * BS, SPAN + n * BS + BS)
                re = full[layer, group, top, 0:SPAN] + full[layer, group, low, SPAN:]
                im = full[layer, group, top, SPAN:] - full[layer, group, low, 0:SPAN]
                block = group * blocks + n
                for part, grad in enumerate((re, im)):
                    grad = grad[:, n * BS : n * BS + BS]
                    row, column = layer * 2 + part, block // 2
                    for at, out in enumerate((mine, other)):

                        @pl.when(lax.axis_index("modes") % 2 == (block + at) % 2)
                        def _():
                            if before:
                                out[row, column] = grad + before[at][row, column]
                            else:
                                out[row, column] = grad


def dense_kernel(
    first,
    limits,
    base,
    cotangent,
    back,
    inverse_turned,
    inverse,
    vectors,
    hidden_bias,
    mine,
    other,
    *rest,
):
    output, hidden, upper, tokens, grad_low, grad_back, middle, sums, upper_sums = rest[-13:-4]
    lower, grad_tokens, units, factors = rest[-4:]
    step, steps = pl.program_id(1), pl.num_programs(1)
    mask = valid_rows(limits[first + pl.program_id(0)], base.shape[0])

    @pl.when(step == 0)
    def _():
        total = base[...] + dot(inverse_turned[...], back[...].reshape(inverse.shape[0], -1))
        middle[...] = total
        unit, factor = norm_forward(total)
        units[...] = unit
        factors[...] = jnp.broadcast_to(factor, factors.shape)
        tokens[...] = (unit * vectors[2:3, :] + vectors[3:4, :]).astype(BF16)
        grad_low[...] = only(mask, cotangent[...].astype(F32)).astype(BF16)
        lower[...] = jnp.zeros_like(lower)
        grad_tokens[...] = jnp.zeros_like(grad_tokens)

    @pl.when((step == 0) & (pl.program_id(0) == 0))
    def _():
        sums[...] = jnp.zeros_like(sums)

    dots = [
        (dot_nt(tokens[...], half[0]), dot_nt(grad_low[...], half[1])) for half in (mine, other)
    ]
    values, grads = [], []
    for half, (upper_in, grad_hidden) in enumerate(dots):
        value, slope = gelu_pair(upper_in + hidden_bias[half])
        grad_upper = grad_hidden * slope
        values.append(value.astype(BF16))
        grads.append(grad_upper.astype(BF16))
        hidden[half] = values[half]
        upper[half] = grads[half]
        upper_sums[half] = jnp.sum(grad_upper, axis=0, keepdims=True)

    def joined(parts, axis):
        return jnp.concatenate(parts, axis=axis)

    lower[...] += dot(joined(values, 1), joined([mine[1], other[1]], 0))
    grad_tokens[...] += dot(joined(grads, 1), joined([mine[0], other[0]], 0))

    @pl.when(step == steps - 1)
    def _():
        total = middle[...]
        output[...] = only(mask, total + lower[...] + vectors[8:9, :]).astype(BF16)
        unit, factor = units[...], factors[:, 0:1]
        grad = grad_tokens[...]
        grad_out = grad_low[...].astype(F32)
        sums[0:1, :] += jnp.sum(grad * unit, axis=0, keepdims=True)
        sums[1:2, :] += jnp.sum(grad, axis=0, keepdims=True)
        sums[2:3, :] += jnp.sum(grad_out, axis=0, keepdims=True)
        through = grad_out + norm_backward(grad, unit, factor, vectors[2:3, :])
        middle[...] = through
        turned = dot(inverse[...], through.astype(BF16))
        grad_back[...] = turned.astype(BF16).reshape(grad_back.shape)


def weight_grad_kernel(groups, *refs):
    up, down = None, None
    for g in range(groups):
        hidden, upper, tokens, grad_low = refs[4 * g : 4 * g + 4]

        def flat(ref):
            return ref[...].reshape(-1, ref.shape[-1])

        up_part = dot_tn(flat(upper), flat(tokens))
        down_part = dot_tn(flat(hidden), flat(grad_low))
        up = up_part if up is None else up + up_part
        down = down_part if down is None else down + down_part
    rest = refs[4 * groups :]
    if len(rest[-1].shape) == 2:
        rest[-2][...] = up.astype(BF16)
        rest[-1][...] = down.astype(BF16)
    else:
        blocks, _, units, features = rest[-1].shape
        for part, grads in enumerate((up, down)):
            grads = grads + rest[part][...].astype(F32)
            rest[-1][:, part] = grads.astype(BF16).reshape(blocks, units, features)


def pack_kernel(early, dense_raw, own, *rest):
    out = rest[-1]
    out[...] = early[...]
    first = rest[0][0:2, :]
    for sums in rest[1:-1]:
        first = first + sums[0:2, :]
    out[0:2, :] = first
    squares = jnp.square(dense_raw[0].astype(F32)) + jnp.square(dense_raw[1].astype(F32))
    out[13:14, :] = jnp.sum(squares, axis=0, keepdims=True)
    out[14:15, 0:BS] = jnp.sum(jnp.square(own[...]), axis=0, keepdims=True)


def input_kernel(first, limits, patches, spread, table_turned, vectors, grad_middle, *rest):
    out, sums = rest[-2:]
    count = limits[first + pl.program_id(0)]
    mask = valid_rows(count, patches.shape[0])

    @pl.when(pl.program_id(0) == 0)
    def _():
        sums[...] = jnp.zeros_like(sums)

    unit, factor = norm_forward(only(mask, patches[...].astype(F32)))
    through = grad_middle[...]
    narrow = dot(table_turned[...], spread[...].reshape(table_turned.shape[1], -1))
    grad_normed = only(mask, through + narrow)
    sums[0:1, :] += jnp.sum(grad_normed * unit, axis=0, keepdims=True)
    sums[1:2, :] += jnp.sum(grad_normed, axis=0, keepdims=True)
    start = through + norm_backward(grad_normed, unit, factor, vectors[0:1, :])
    out[...] = only(mask, start).astype(BF16)


def update_kernel(halves, late, *refs):
    dense_raw, dense_old, refs = refs[0], refs[1:4], refs[4:]
    spectral_raw, refs = refs[:halves], refs[halves:]
    spectral_old, vector_old, refs = refs[0:3], refs[3:6], refs[6:]
    norm, dense_out, spectral_out, vector_out = refs[0], refs[1:5], refs[5:9], refs[9:13]
    vector_raw = late[0:13, :]
    squares = jnp.sum(vector_raw * vector_raw, axis=1, keepdims=True)
    squares = jnp.sum(squares, axis=0, keepdims=True)
    for row in (13, 14):
        squares = squares + jnp.sum(late[row : row + 1, :], axis=1, keepdims=True)
    grad_norm = jnp.sqrt(squares)
    factor = jnp.minimum(1.0, CLIP_LEVEL / (grad_norm + 1e-06))
    norm[...] = grad_norm

    def update(raw, old, out, at, rate, decay):
        grad = raw.astype(F32) * factor.reshape((1,) * raw.ndim)
        news = adam_update(*(ref[at] for ref in old), grad, rate, decay)
        for ref, value in zip(out, (grad,) + news):
            ref[at] = value

    for part in range(2):
        at = (slice(None), part, slice(None))
        update(dense_raw[part], dense_old, dense_out, at, RATE_MATRIX, DECAY_MATRIX)
    if halves == 1:
        update(spectral_raw[0][...], spectral_old, spectral_out, ..., RATE_MATRIX, DECAY_MATRIX)
    else:
        core = lax.axis_index("modes") % 2
        for half, raw in enumerate(spectral_raw):
            for z in range(raw.shape[0]):
                at = pl.ds(2 * z + (core ^ half), 1)
                update(raw[z : z + 1], spectral_old, spectral_out, at, RATE_MATRIX, DECAY_MATRIX)

    @pl.when(pl.program_id(0) == 0)
    def _():
        update(vector_raw, vector_old, vector_out, ..., RATE_VECTOR, 0.0)


def update_call(late, dense_raw, dense_old, spectral_raw, spectral_old, vector_old):
    steps = 4
    units, _, features = dense_old[0].shape
    spectral_shape = spectral_old[0].shape
    spectral_old = [old.reshape(32, BS, BS) for old in spectral_old]
    dense = pl.BlockSpec((units // steps, 2, features), lambda i: (i, 0, 0))
    raw = pl.BlockSpec((2, units // steps, features), lambda i: (0, i, 0))
    if units // steps % 8:
        raw = dense = None
    if dense is None:
        dense, raw = whole(dense_old[0]), whole(dense_raw)
    spectral = pl.BlockSpec((8, BS, BS), lambda i: (i, 0, 0))
    blocks = spectral_raw[0].shape[1]
    sums = pl.BlockSpec((None, blocks, BS, BS), lambda i: (i, 0, 0, 0))
    vector = whole(vector_old[0])
    out = pl.pallas_call(
        functools.partial(update_kernel, len(spectral_raw)),
        grid=(steps,),
        in_specs=[whole(late), raw]
        + [dense] * 3
        + [sums] * len(spectral_raw)
        + [spectral] * 3
        + [vector] * 3,
        out_specs=[pl.BlockSpec((1, 1), lambda i: (0, 0))]
        + [dense] * 4
        + [spectral] * 4
        + [vector] * 4,
        out_shape=[
            jax.ShapeDtypeStruct(shape, F32)
            for shape in [(1, 1)]
            + [dense_old[0].shape] * 4
            + [(32, BS, BS)] * 4
            + [vector_old[0].shape] * 4
        ],
        compiler_params=params(),
        cost_estimate=cost(0, 32 * (dense_raw.size + 32 * BS * BS)),
        name="update",
    )(late, dense_raw, *dense_old, *spectral_raw, *spectral_old, *vector_old)
    spectral_new = [new.reshape(spectral_shape) for new in out[5:9]]
    return (out[0].reshape(()), *out[1:5], *spectral_new, *out[9:13])


def split_blocks(values):
    return values.reshape(values.shape[:-1] + (NB, BS))


def block_mix(values, matrix):
    mixed = jnp.einsum(
        "ckpsni,pqnij->ckqsnj", split_blocks(values), matrix, preferred_element_type=F32
    )
    return mixed.reshape(values.shape)


def complex_matrix(weights):
    return jnp.stack([jnp.stack([weights[0], weights[1]]), jnp.stack([-weights[1], weights[0]])])


def fold_complex(grad_matrix):
    return jnp.stack([grad_matrix[0, 0] + grad_matrix[1, 1], grad_matrix[0, 1] - grad_matrix[1, 0]])


def shrink(values):
    return values - SHRINK_LEVEL * jnp.tanh(values / SHRINK_LEVEL)


def plain_filter(received, mixes, biases, keep, tables):
    band_count, crops, rows, features = received.shape
    rows_in = received.reshape(band_count, crops, 2, rows // 2, features)
    modes = jnp.einsum("pjqh,hcqsd->cjpsd", tables[0], rows_in, preferred_element_type=F32)
    modes = modes.astype(BF16)
    pre_active = block_mix(modes, mixes[0]) + biases[0]
    active = jax.nn.gelu(pre_active).astype(BF16)
    pre_shrink = block_mix(active, mixes[1]) + biases[1]
    shrunk = (shrink(pre_shrink) * keep).astype(BF16)
    back = jnp.einsum("phqj,cjqsd->hcpsd", tables[1], shrunk, preferred_element_type=F32)
    return ((modes, pre_active, pre_shrink), back.astype(BF16).reshape(received.shape))


def plain_filter_back(received, saved, mixes, keep, tables):
    modes, pre_active, pre_shrink = saved
    band_count, crops, rows, features = received.shape
    grads = received.reshape(band_count, crops, 2, rows // 2, features)
    grad_shrunk = jnp.einsum("phqj,hcpsd->cjqsd", tables[1], grads, preferred_element_type=F32)
    grad_shrink = jax.vjp(shrink, pre_shrink)[1](grad_shrunk * keep)[0]
    shrink_low = grad_shrink.astype(BF16)
    active_value, active_pull = jax.vjp(jax.nn.gelu, pre_active)
    pairs = "chpsni,chqsnm->pqnim"
    grad_second = jnp.einsum(
        pairs,
        split_blocks(active_value.astype(BF16)),
        split_blocks(shrink_low),
        preferred_element_type=F32,
    )
    back = "cjqsnk,pqnik->cjpsni"
    grad_active = jnp.einsum(
        back, split_blocks(shrink_low), mixes[1], preferred_element_type=F32
    ).reshape(pre_active.shape)
    grad_first = active_pull(grad_active)[0]
    first_low = grad_first.astype(BF16)
    grad_one = jnp.einsum(
        pairs, split_blocks(modes), split_blocks(first_low), preferred_element_type=F32
    )
    grad_modes = jnp.einsum(
        back, split_blocks(first_low), mixes[0], preferred_element_type=F32
    ).reshape(pre_active.shape)
    spread = jnp.einsum(
        "pjqh,cjpsd->hcqsd", tables[0], grad_modes.astype(BF16), preferred_element_type=F32
    )
    weights = jnp.stack([fold_complex(grad_one), fold_complex(grad_second)])
    sums = jnp.concatenate(
        [jnp.sum(grad_first, axis=(0, 1, 3)), jnp.sum(grad_shrink, axis=(0, 1, 3))]
    )
    return (spread.astype(BF16).reshape(received.shape), weights, sums)


def on_device(
    patches,
    cotangent,
    heights,
    widths,
    band_lengths,
    dense_master,
    dense_first,
    dense_second,
    spectral_master,
    spectral_first,
    spectral_second,
    vector_master,
    vector_first,
    vector_second,
):
    band_count = lax.axis_size("modes")
    my_band = lax.axis_index("modes")
    micros = patches.shape[0]
    cells, features = patches.shape[3:]
    wave_count = cells // 2
    slots = wave_count // band_count
    rows = 2 * slots
    hidden_units = 4 * features
    direct = band_count == 8 and slots % 16 == 0
    groups = [[0, 1], [2, 3]] if micros == 4 else [[m] for m in range(micros)]
    spans = features // SPAN

    kept_count = jnp.minimum(jnp.sum(band_lengths), wave_count)
    counts = jnp.where(my_band < heights[:, 0], widths[:, 0], 0)
    limits = jnp.concatenate(
        [counts, jnp.stack([my_band * slots, kept_count]).astype(jnp.int32)]
    ).astype(jnp.int32)
    forward, forward_turned, inverse, inverse_turned = wave_tables(band_count, cells)

    core = my_band % 2
    core_groups = [list(range(c, band_count, 2)) for c in range(2)]
    four = band_count == 8 and lax.axis_size("dp") == 4
    mine = dense_master.transpose(1, 0, 2).astype(BF16)
    mine = lax.all_gather(mine, "modes", axis=1, tiled=True, axis_index_groups=core_groups)
    half_units = hidden_units // 2

    def by_core(values, back=False):
        units = dense_master.shape[0]
        if back:
            values = jnp.where(core == 0, values, values[::-1]).reshape(2, -1, units)
            return values.transpose(1, 0, 2).reshape(-1)
        values = values.reshape(-1, 2, units).transpose(1, 0, 2).reshape(2, 1, half_units)
        return jnp.where(core == 0, values, values[::-1])

    hidden_bias = by_core(vector_master[9:13].reshape(-1))

    def exchange(values):
        return lax.all_to_all(values, "modes", split_axis=0, concat_axis=0, tiled=True)

    def micro_spec(group):
        return pl.BlockSpec(
            (None, None, None, cells, features), lambda g, *_: (group[0] + g, 0, 0, 0, 0)
        )

    def sent(group):
        if direct:
            return (
                jax.ShapeDtypeStruct((band_count, len(group), rows, features), BF16),
                pl.BlockSpec((band_count, None, rows, features), lambda g, *_: (0, g, 0, 0)),
            )
        return (
            jax.ShapeDtypeStruct((len(group), cells, features), BF16),
            pl.BlockSpec((None, cells, features), lambda g, *_: (g, 0, 0)),
        )

    def to_wire(values):
        if direct:
            return values
        return values.reshape(-1, band_count, rows, features).transpose(1, 0, 2, 3)

    def from_wire(values):
        if direct:
            return values
        return values.transpose(1, 0, 2, 3).reshape(-1, cells, features)

    matmul_flops = 2 * cells * cells * features
    cell_bytes = cells * features

    def spread_call(group):
        shape, spec = sent(group)
        per_micro = pl.BlockSpec((None, cells, features), lambda g: (g, 0, 0))
        out, base = pl.pallas_call(
            functools.partial(spread_kernel, group[0]),
            grid=(len(group),),
            in_specs=[SMEM, SMEM, micro_spec(group), whole(forward), whole(vector_master)],
            out_specs=[spec, per_micro],
            out_shape=[shape, jax.ShapeDtypeStruct((len(group), cells, features), F32)],
            compiler_params=params(),
            cost_estimate=cost(len(group) * matmul_flops, len(group) * 8 * cell_bytes),
            name="spread_rows",
        )(heights.reshape(-1), widths.reshape(-1), patches, forward, vector_master)
        return (to_wire(out), base)

    if direct:
        mixes = pl.pallas_call(
            mix_kernel,
            grid=(2,),
            in_specs=[pl.BlockSpec((None, 2, NB, BS, BS), lambda i: (i, 0, 0, 0, 0))],
            out_specs=pl.BlockSpec((None, spans, 2 * SPAN, 2 * SPAN), lambda i: (i, 0, 0, 0)),
            out_shape=jax.ShapeDtypeStruct((2, spans, 2 * SPAN, 2 * SPAN), BF16),
            compiler_params=params(SMALL),
            cost_estimate=cost(0, 16 * NB * BS * BS * 4),
            name="build_mix",
        )(spectral_master)
        biases = vector_master[4:8].reshape(2, 2, spans, SPAN).transpose(0, 2, 1, 3)
        biases = biases.reshape(2, spans, 1, 2 * SPAN)
    else:
        low = spectral_master.astype(BF16)
        mixes = (complex_matrix(low[0]), complex_matrix(low[1]))
        biases = (
            vector_master[4:6][None, None, :, None, :],
            vector_master[6:8][None, None, :, None, :],
        )
        tables = row_tables(band_count)
        keep = (my_band * slots + jnp.arange(slots, dtype=jnp.int32) < kept_count).astype(F32)
        keep = keep[None, None, None, :, None]
    mode_rows = 8 * slots
    mix_flops = 2 * mode_rows * (2 * SPAN) * (2 * SPAN) * spans

    def filter_call(group, received):
        if not direct:
            return plain_filter(received, mixes, biases, keep, tables)
        shape, _ = sent(group)
        saved = jax.ShapeDtypeStruct((spans, len(group) * mode_rows, 2 * SPAN), BF16)
        modes, back = pl.pallas_call(
            functools.partial(filter_kernel, slots, micros),
            in_specs=[SMEM, VMEMS, VMEMS, VMEMS],
            out_shape=[saved, shape],
            scratch_shapes=[pltpu.VMEM(saved.shape, BF16)],
            compiler_params=params(),
            cost_estimate=cost(len(group) * 2 * mix_flops, len(group) * 6 * cell_bytes),
            name="filter_modes",
        )(limits, received, mixes, biases)
        return (modes, back)

    def filter_back_call(group, received, saved, ahead, before):
        if not direct:
            return plain_filter_back(received, saved, mixes, keep, tables)
        shape, _ = sent(group)
        blocks = jax.ShapeDtypeStruct((4, 4, BS, BS), F32)
        spread, sums, mine, other = pl.pallas_call(
            lambda *refs: filter_back_kernel(slots, micros, *refs[: 5 + len(before)], *refs[6 + len(before) :]),
            in_specs=[SMEM] + [VMEMS] * (4 + len(before)) + [HBM],
            out_shape=[
                shape,
                jax.ShapeDtypeStruct((spans, 8, 2 * SPAN), F32),
                blocks,
                blocks,
            ],
            scratch_shapes=[
                pltpu.VMEM((2, spans, 2 * SPAN, 2 * SPAN), F32),
                pltpu.VMEM((spans, len(group) * mode_rows, 2 * SPAN), F32),
            ],
            compiler_params=params(),
            cost_estimate=cost(1 + len(before) * 10**11, 1),
            name="filter_modes_back",
        )(limits, received, saved, mixes, biases, *before, ahead)
        sums = sums[:, 0:2].reshape(spans, 2, 2, SPAN).transpose(1, 2, 0, 3).reshape(4, features)
        return (spread, (mine, other), sums)

    tile = 512

    def dense_call(group, base, back, output):
        shape, spec = sent(group)
        count = len(group)
        per_micro = pl.BlockSpec((None, cells, features), lambda g, t: (g, 0, 0))
        per_tile = pl.BlockSpec((2, None, cells, tile), lambda g, t: (0, g, 0, t))
        per_half = pl.BlockSpec((2, tile, features), lambda g, t: (0, t, 0))
        previous = [] if output is None else [output]
        operands = [
            limits,
            base,
            cotangent,
            back,
            inverse_turned,
            inverse,
            vector_master,
            hidden_bias,
            mine,
            other,
        ]
        whole_low = jax.ShapeDtypeStruct((count, cells, features), BF16)
        whole_full = jax.ShapeDtypeStruct((count, cells, features), F32)
        sums = jax.ShapeDtypeStruct((8, features), F32)
        tiled = jax.ShapeDtypeStruct((2, count, cells, half_units), BF16)
        return pl.pallas_call(
            functools.partial(dense_kernel, group[0]),
            grid=(count, half_units // tile),
            in_specs=[
                SMEM,
                per_micro,
                micro_spec(group),
                spec,
                whole(inverse_turned),
                whole(inverse),
                whole(vector_master),
                pl.BlockSpec((2, 1, tile), lambda g, t: (0, 0, t)),
                per_half,
                per_half,
            ]
            + [ANY for _ in previous],
            out_specs=[
                micro_spec(group),
                per_tile,
                per_tile,
                per_micro,
                per_micro,
                spec,
                per_micro,
                whole(sums),
                pl.BlockSpec((2, None, 1, tile), lambda g, t: (0, g, 0, t)),
            ],
            out_shape=[
                jax.ShapeDtypeStruct(patches.shape, BF16),
                tiled,
                tiled,
                whole_low,
                whole_low,
                shape,
                whole_full,
                sums,
                jax.ShapeDtypeStruct((2, count, 1, half_units), F32),
            ],
            scratch_shapes=[pltpu.VMEM((cells, features), F32) for _ in range(3)]
            + [pltpu.VMEM((cells, LANES), F32)],
            input_output_aliases={len(operands): 0} if previous else {},
            compiler_params=params(),
            cost_estimate=cost(
                count * 8 * cells * features * hidden_units,
                count * (20 * cell_bytes + 4 * cells * hidden_units)
                + 4 * features * hidden_units * count,
            ),
            name="dense_both_ways",
        )(*operands, *previous)

    chunk = half_units // 4
    own_units = dense_master.shape[0]

    def weight_grad_call(saved, half, received, ahead):
        specs, operands = [], []
        for hidden, upper, tokens, grad_low in saved:
            per_chunk = pl.BlockSpec(
                (None, hidden.shape[1], cells, chunk), lambda t: (half, 0, 0, t)
            )
            specs += [per_chunk, per_chunk, whole(tokens), whole(grad_low)]
            operands += [hidden, upper, tokens, grad_low]
        single = pl.BlockSpec((chunk, features), lambda t: (t, 0))
        out_specs = [single] * 2
        out_shape = [jax.ShapeDtypeStruct((half_units, features), BF16)] * 2
        if received:
            owners = chunk // own_units
            out_specs = pl.BlockSpec((owners, 2, own_units, features), lambda t: (t, 0, 0, 0))
            out_shape = jax.ShapeDtypeStruct((4 * owners, 2, own_units, features), BF16)
        return pl.pallas_call(
            functools.partial(weight_grad_kernel, len(saved)),
            grid=(4,),
            in_specs=specs + [single] * len(received) + [ANY] * len(ahead),
            out_specs=out_specs,
            out_shape=out_shape,
            compiler_params=params(),
            cost_estimate=cost(1, 1 if received else 16 * micros * cell_bytes),
            name="dense_weight_grads",
        )(*operands, *received, *ahead)

    def input_call(group, spread, grad_middle, input_grad, ahead):
        _, spec = sent(group)
        previous = [] if input_grad is None else [input_grad]
        operands = [limits, patches, spread, forward_turned, vector_master, grad_middle]
        operands += ahead
        return pl.pallas_call(
            functools.partial(input_kernel, group[0]),
            grid=(len(group),),
            in_specs=[
                SMEM,
                micro_spec(group),
                spec,
                whole(forward_turned),
                whole(vector_master),
                pl.BlockSpec((None, cells, features), lambda g: (g, 0, 0)),
            ]
            + [HBM for _ in ahead]
            + [ANY for _ in previous],
            out_specs=[micro_spec(group), pl.BlockSpec((8, features), lambda g: (0, 0))],
            out_shape=[
                jax.ShapeDtypeStruct(patches.shape, BF16),
                jax.ShapeDtypeStruct((8, features), F32),
            ],
            input_output_aliases={len(operands): 0} if previous else {},
            compiler_params=params(),
            cost_estimate=cost(len(group) * matmul_flops, len(group) * 11 * cell_bytes),
            name="input_grads",
        )(*operands, *previous)

    def exchange_all(values):
        done = []
        for value, others in values:
            done.append(exchange(tie(value, *done[-1:], *others) if done or others else value))
        return done

    spread, bases = zip(*[spread_call(group) for group in groups])
    received = exchange_all([(values, ()) for values in spread])
    mine = lax.all_gather(tie(mine, received[0], spread[1]), "dp", axis=1, tiled=True)
    filtered = [filter_call(group, got) for group, got in zip(groups, received)]
    returned = exchange_all([(back, received[-1:]) for _, back in filtered])
    mine = tie(mine, returned[0], jax.tree.leaves(filtered[-1][0])[0])
    other = swap(mine, "modes", 1)
    output, dense_parts = None, []
    for group, back, base in zip(groups, returned, bases):
        dense_parts.append(dense_call(group, base, from_wire(back), output))
        output = dense_parts[-1][0]
    received = exchange_all([(to_wire(part[5]), returned[-1:]) for part in dense_parts])
    saved_parts = [part[1:5] for part in dense_parts]
    turned, ahead = [], received[0]
    for group, got, (saved, _) in zip(groups, received, filtered):
        before = turned[-1][1] if turned and direct else ()
        turned.append(filter_back_call(group, got, saved, ahead, before))
        if len(turned) == 1:
            other_grads = weight_grad_call(saved_parts, 1, (), jax.tree.leaves(turned[0][1])[:1])
            other_grads = [swap(grads, "modes", 1) for grads in other_grads]
            after = [received[-1], jax.tree.leaves(turned[0][1])[0]]
            dense_raw = weight_grad_call(saved_parts, 0, other_grads, after)
            ahead = dense_raw
    returned = exchange_all([(part[0], (received[-1],)) for part in turned])
    dense_raw = lax.psum_scatter(dense_raw, "dp", scatter_dimension=0, tiled=True)
    dense_sums = sum(part[7] for part in dense_parts)
    early = jnp.concatenate(
        [
            jnp.zeros((2, features), F32),
            dense_sums[0:2],
            sum(part[2] for part in turned),
            dense_sums[2:3],
            by_core(sum(jnp.sum(part[8], axis=1) for part in dense_parts), True).reshape(-1, features),
            jnp.zeros((3, features), F32),
        ]
    )

    input_grad, input_sums = None, []
    if four:
        spectral_parts = scatter_spectral(*turned[-1][1])
        spectral_own = own_spectral(spectral_parts)
    else:
        spectral_parts = returned
    for group, spread, part in zip(groups, returned, dense_parts):
        ahead = [spectral_own] if four and group == groups[-1] else [early]
        input_grad, sums = input_call(group, from_wire(spread), part[6], input_grad, ahead)
        input_sums.append(sums)
    dense_raw = lax.psum_scatter(
        tie(dense_raw, returned[-1], input_sums[0], spectral_parts[-1]),
        "modes",
        scatter_dimension=0,
        tiled=True,
        axis_index_groups=core_groups,
    )[0]
    def pack(own):
        return pick_call(
            pack_kernel,
            jax.ShapeDtypeStruct(early.shape, F32),
            early,
            dense_raw,
            own,
            *input_sums,
            name="pack_sums",
        )

    if four:
        spectral_sum = gather_spectral(spectral_own, input_sums[-1])
        late = pack(tie(spectral_own, spectral_sum[0]))
        late = late + swap(late, "modes", 1)
        late = sum_four(late, "dp", 1)
        late = sum_four(late, "modes", 2)
    else:
        if direct:
            even, odd = (jnp.where(core == c, *turned[-1][1]) for c in range(2))
            spectral_raw = jnp.stack([even, odd], axis=2)
        else:
            spectral_raw = sum(part[1] for part in turned)
        spectral_sum = [lax.psum(spectral_raw, ("dp", "modes")).reshape(4, 8, BS, BS)]
        late = pack(jnp.zeros((BS, BS), F32))
        late = lax.psum(late, ("dp", "modes"))
        squares = jnp.sum(spectral_sum[0] * spectral_sum[0])
        late = jnp.concatenate([late[:15], jnp.zeros((1, features), F32)]).at[14].add(squares / features)
    updated = update_call(
        late,
        dense_raw,
        (dense_master, dense_first, dense_second),
        spectral_sum,
        (spectral_master, spectral_first, spectral_second),
        (vector_master, vector_first, vector_second),
    )
    return (output, input_grad) + updated


def solution(mesh):
    return jax.shard_map(
        on_device,
        mesh=mesh,
        in_specs=(
            P(None, "dp", "modes", None, None),
            P(None, "dp", "modes", None, None),
            P(None, "dp"),
            P(None, "dp"),
            P(),
            P(("dp", "modes"), None, None),
            P(("dp", "modes"), None, None),
            P(("dp", "modes"), None, None),
            P(),
            P(),
            P(),
            P(),
            P(),
            P(),
        ),
        out_specs=(
            P(None, "dp", "modes", None, None),
            P(None, "dp", "modes", None, None),
            P(),
            P(("dp", "modes"), None, None),
            P(("dp", "modes"), None, None),
            P(("dp", "modes"), None, None),
            P(("dp", "modes"), None, None),
            P(),
            P(),
            P(),
            P(),
            P(),
            P(),
            P(),
            P(),
        ),
        check_vma=False,
    )
```

time: 1290 us -> 465 us (0.36)
  matrix products: 323 us -> 0 us
  waiting for transfers between devices: 432 us -> 156 us
  local copies, waits for them, and re-layouts: 284 us -> 11.5 us
  Pallas kernels: 0 us -> 197 us
  other arithmetic: 108 us -> 4.29 us
  blocking collectives: 39.9 us -> 0 us
    dot_general x80 -> x0, matrix products: 323 us -> none  [the longest x4 39.8 us: on_device(): jnp.einsum('td,fd->tf', grad_low, weight_down, preferred_element_type=jnp...]
    all_to_all x16 -> x8, waiting for transfers between devices: 319 us -> 75.5 us  [exchange(): lax.all_to_all(values, 'modes', split_axis=0, concat_axis=0, tiled=True)]
    pallas_call x0 -> x31, Pallas kernels: none -> 197 us  [the longest x2 74.2 us: dense_call(): pl.pallas_call(functools.partial(dense_kernel, group[0]), grid=(count, ha...]
    reduce_scatter x1 -> x2, waiting for transfers between devices: 113 us -> 0.01 us  [the longest x1 0.01 us: on_device(): lax.psum_scatter(dense_raw, 'dp', scatter_dimension=0, tiled=True)]
    reshape x32 -> x5, local copies, waits for them, and re-layouts: 103 us -> 0.82 us  [the longest x1 0.62 us: on_device(): biases = biases.reshape(2, spans, 1, 2 * SPAN)]
    unnamed x480 -> x59, local copies, waits for them, and re-layouts: 68.1 us -> 8.88 us
    all_gather x1 -> x2, waiting for transfers between devices: 0.02 us -> 50.1 us  [the longest x1 50.1 us: on_device(): lax.all_gather(mine, 'modes', axis=1, tiled=True, axis_index_groups=core_...]
    psum x1 -> x0, blocking collectives: 39.9 us -> none  [on_device(): lax.psum((spectral_acc, vector_acc, jnp.sum(dense_grad * dense_grad)), ('...]
  transfers between devices with their start and end apart: 19 -> 36, of which waited for: 16 -> 23; matrix products, arithmetic and copies ran while one was open for 38% -> 2% of each run, Pallas kernels for 0% -> 40%
where the time goes in v1:
time: 465 us; the launch traced here: 456 us
  Pallas kernels  197 us (42%)
  waiting for transfers between devices  156 us (34%)
  starting transfers between devices  72.7 us (16%)
  between operations  15.4 us (3%)
  local copies, waits for them, and re-layouts  11.5 us (2%)
    all_to_all x8, waiting for transfers between devices, exchange(): lax.all_to_all(values, 'modes', split_axis=0, concat_axis=0, tiled=True)  75.5 us
    pallas_call x2, Pallas kernels, dense_call(): pl.pallas_call(functools.partial(dense_kernel, group[0]), grid=(count, ha...  74.2 us
    all_gather x1, waiting for transfers between devices, on_device(): lax.all_gather(mine, 'modes', axis=1, tiled=True, axis_index_groups=core_...  50.1 us
    all_to_all x8, starting transfers between devices, exchange(): lax.all_to_all(values, 'modes', split_axis=0, concat_axis=0, tiled=True)  45.9 us
    pallas_call x2, Pallas kernels, filter_back_call(): pl.pallas_call(lambda *refs: filter_back_kernel(slots, micros, *refs[:5 +...  33.4 us
    pallas_call x2, Pallas kernels, weight_grad_call(): pl.pallas_call(functools.partial(weight_grad_kernel, len(saved)), grid=(4...  31.8 us
    ppermute x24, waiting for transfers between devices, swap(): return lax.ppermute(values, axis, [(i, i ^ mask) for i in range(count)])  29.9 us
    ppermute x24, starting transfers between devices, swap(): return lax.ppermute(values, axis, [(i, i ^ mask) for i in range(count)])  26.5 us
  transfers between devices with their start and end apart: 36, of which 23 were waited for; matrix products, arithmetic and copies ran while one was open for 2% of the time, Pallas kernels for 40%

profile of v1, /device:TPU:0, one launch (start us, length us, event | category | flops | bytes accessed | tf_op | source)
XLA Modules:
  0.0 456.4 jit_solution(8645396840758748022)
XLA Ops:
  7.2 5.0 %spread_rows.3 = (bf16[8,2,64,768]{3,2,1,0:T(8,128)(2,1)}, f32[2,512,768]{2,1,0:T(8,128)}) custom-call(s32[4]{0:T(128)} %bitcast.42, s32[4]{0:T(128)} %bitcast.40, bf16[4,1,1,512,768]{4,3,2,1,0:T(8,128)(2,1)} %patches.7, bf16[512,512]{1,0:T(8,128)(2,1)} %constant.34.clone.table, f32[13,768]{1,0:T(8,128)} %refs_9_.1), custom_call_target="tpu_custom_call" | custom-call | flops 805306368 | bytes 6291456 | tf_op jit(solution)/shard_map/spread_rows/pallas_call | solution.py:773
  12.1 6.5 %all-to-all-start = ((bf16[8,2,64,768]{3,2,1,0:T(8,128)(2,1)}), bf16[8,2,64,768]{3,2,1,0:T(8,128)(2,1)}, u32[]{:S(2)}, u32[]{:S(2)}) async-start(bf16[8,2,64,768]{3,2,1,0:T(8,128)(2,1)} %get-tuple-element.78), calls=%async_computation | async-start | bytes 3145728 | tf_op jit(solution)/shard_map/all_to_all | solution.py:739
  19.5 5.0 %spread_rows.2 = (bf16[8,2,64,768]{3,2,1,0:T(8,128)(2,1)}, f32[2,512,768]{2,1,0:T(8,128)}) custom-call(s32[4]{0:T(128)} %bitcast.43, s32[4]{0:T(128)} %bitcast.41, bf16[4,1,1,512,768]{4,3,2,1,0:T(8,128)(2,1)} %patches.7, bf16[512,512]{1,0:T(8,128)(2,1)} %constant.34.clone.table, f32[13,768]{1,0:T(8,128)} %refs_9_.1), custom_call_target="tpu_custom_call" | custom-call | flops 805306368 | bytes 6291456 | tf_op jit(solution)/shard_map/spread_rows/pallas_call | solution.py:773
  24.5 50.1 %all-gather.3.cloned.1.call-done.__0_ = bf16[2,384,768]{2,1,0:T(8,128)(2,1)} async-done(((bf16[2,96,768]{2,1,0:T(8,128)(2,1)}), bf16[2,384,768]{2,1,0:T(8,128)(2,1)}) %all-gather.3.cloned.1.call-update) | async-done | bytes 1179664 | tf_op jit(solution)/shard_map/all_gather | solution.py:725
  74.6 0.9 all-to-all-done.__1_.received
  75.6 4.4 all-to-all-start.1
  80.7 0.9 build_mix.1.mix.refs_3_
  81.6 2.2 copy-done
  85.8 8.1 %filter_modes.3 = (bf16[2,512,768]{2,1,0:T(8,128)(2,1)}, bf16[8,2,64,768]{3,2,1,0:T(8,128)(2,1)}) custom-call(s32[6]{0:T(128)} %pad_add_fusion.limits.refs_0_, bf16[8,2,64,768]{3,2,1,0:T(8,128)(2,1)} %all-to-all-done.__1_.received, bf16[2,2,768,768]{3,2,1,0:T(8,128)(2,1)} %copy-done, f32[2,2,1,768]{3,2,1,0:T(1,128)} %reshape.96.bias.refs_4_), custom_call_target="tpu_custom_call" | custom-call | flops 2415919104 | bytes 4718592 | tf_op jit(solution)/shard_map/filter_modes/pallas_call | solution.py:816
  93.9 24.0 %all-to-all-done.1.received.__1_.__2_ = bf16[8,2,64,768]{3,2,1,0:T(8,128)(2,1)} async-done(((bf16[8,2,64,768]{3,2,1,0:T(8,128)(2,1)}), bf16[8,2,64,768]{3,2,1,0:T(8,128)(2,1)}, u32[]{:S(2)}, u32[]{:S(2)}) %all-to-all-start.1) | async-done | bytes 1572896 | tf_op jit(solution)/shard_map/all_to_all | solution.py:739
  117.9 4.3 all-to-all-start.2
  122.2 8.1 %filter_modes.2 = (bf16[2,512,768]{2,1,0:T(8,128)(2,1)}, bf16[8,2,64,768]{3,2,1,0:T(8,128)(2,1)}) custom-call(s32[6]{0:T(128)} %pad_add_fusion.limits.refs_0_, bf16[8,2,64,768]{3,2,1,0:T(8,128)(2,1)} %all-to-all-done.1.received.__1_.__2_, bf16[2,2,768,768]{3,2,1,0:T(8,128)(2,1)} %copy-done, f32[2,2,1,768]{3,2,1,0:T(1,128)} %reshape.96.bias.refs_4_), custom_call_target="tpu_custom_call" | custom-call | flops 2415919104 | bytes 4718592 | tf_op jit(solution)/shard_map/filter_modes/pallas_call | solution.py:816
  130.2 29.8 %all-to-all-done.2.__1_.back = bf16[8,2,64,768]{3,2,1,0:T(8,128)(2,1)} async-done(((bf16[8,2,64,768]{3,2,1,0:T(8,128)(2,1)}), bf16[8,2,64,768]{3,2,1,0:T(8,128)(2,1)}, u32[]{:S(2)}, u32[]{:S(2)}) %all-to-all-start.2) | async-done | bytes 1572896 | tf_op jit(solution)/shard_map/all_to_all | solution.py:739
  160.0 4.6 %all-to-all-start.3 = ((bf16[8,2,64,768]{3,2,1,0:T(8,128)(2,1)}), bf16[8,2,64,768]{3,2,1,0:T(8,128)(2,1)}, u32[]{:S(2)}, u32[]{:S(2)}) async-start(bf16[8,2,64,768]{3,2,1,0:T(8,128)(2,1)} %tie.14), calls=%async_computation.3 | async-start | bytes 3145728 | tf_op jit(solution)/shard_map/all_to_all | solution.py:739
  165.4 2.9 collective-permute-done.other
  168.2 37.1 %dense_both_ways.2 = (bf16[4,1,1,512,768]{4,3,2,1,0:T(8,128)(2,1)}, bf16[2,2,512,1536]{3,2,1,0:T(8,128)(2,1)}, bf16[2,2,512,1536]{3,2,1,0:T(8,128)(2,1)}, bf16[2...) custom-call(s32[6]{0:T(128)} %pad_add_fusion.limits.refs_0_, ...), custom_call_target="tpu_custom_call" | custom-call | flops 19327352832 | bytes 47185920 | tf_op jit(solution)/shard_map/dense_both_ways/pallas_call | solution.py:877
  205.3 4.3 all-to-all-start.4
  209.7 37.1 %dense_both_ways.3 = (bf16[4,1,1,512,768]{4,3,2,1,0:T(8,128)(2,1)}, bf16[2,2,512,1536]{3,2,1,0:T(8,128)(2,1)}, bf16[2,2,512,1536]{3,2,1,0:T(8,128)(2,1)}, bf16[2...) custom-call(s32[6]{0:T(128)} %pad_add_fusion.limits.refs_0_, ...), custom_call_target="tpu_custom_call", output_to_operand_aliasing={{0}: (10, {})} | custom-call | flops 19327352832 | bytes 47185920 | tf_op jit(solution)/shard_map/dense_both_ways/pallas_call | solution.py:877
  247.5 12.8 %all-to-all-start.5 = ((bf16[8,2,64,768]{3,2,1,0:T(8,128)(2,1)}), bf16[8,2,64,768]{3,2,1,0:T(8,128)(2,1)}, u32[]{:S(2)}, u32[]{:S(2)}) async-start(bf16[8,2,64,768]{3,2,1,0:T(8,128)(2,1)} %tie.18), calls=%async_computation.5 | async-start | bytes 3145728 | tf_op jit(solution)/shard_map/all_to_all | solution.py:739
  260.3 15.7 %filter_modes_back.2 = (bf16[8,2,64,768]{3,2,1,0:T(8,128)(2,1)}, f32[2,8,768]{2,1,0:T(8,128)}, f32[4,4,96,96]{3,2,1,0:T(8,128)}, f32[4,4,96,96]{3,2,1,0:T(8,128)}) custom-call(s32[6]{0:T(128)} %pad_add_fusion.limits.refs_0_, bf16[8,2,64,768]{3,2,1,0:T(8,128)(2,1)} %all-to-all-done.4.__1_.refs_1_.refs_5_, bf16[2,512,768]{2,1,0:T(8,128)(2,1)} %get-tuple-element.87.refs_2_, ...), custom_call_target="tpu_custom_call" | custom-call | flops 1 | bytes 1 | tf_op jit(solution)/shard_map/filter_modes_back/pallas_call | solution.py:832
  275.9 15.5 %dense_weight_grads.2 = (bf16[1536,768]{1,0:T(8,128)(2,1)}, bf16[1536,768]{1,0:T(8,128)(2,1)}) custom-call(bf16[2,2,512,1536]{3,2,1,0:T(8,128)(2,1)} %get-tuple-element.90.refs_0_, bf16[2,2,512,1536]{3,2,1,0:T(8,128)(2,1)} %get-tuple-element.91.refs_1_, bf16[2,512,768]{2,1,0:T(8,128)(2,1)} %get-tuple-element.92.refs_2_, ...), custom_call_target="tpu_custom_call" | custom-call | flops 1 | bytes 25165824 | tf_op jit(solution)/shard_map/dense_weight_grads/pallas_call | solution.py:945
  291.9 6.0 %all-to-all-done.5.refs_10_.refs_1_.__1_.__2_ = bf16[8,2,64,768]{3,2,1,0:T(8,128)(2,1)} async-done(((bf16[8,2,64,768]{3,2,1,0:T(8,128)(2,1)}), bf16[8,2,64,768]{3,2,1,0:T(8,128)(2,1)}, u32[]{:S(2)}, u32[]{:S(2)}) %all-to-all-start.5) | async-done | bytes 1572896 | tf_op jit(solution)/shard_map/all_to_all | solution.py:739
  298.0 4.3 all-to-all-start.6
  302.5 16.3 %dense_weight_grads.3.refs_7_ = bf16[16,2,96,768]{3,2,1,0:T(8,128)(2,1)} custom-call(bf16[2,2,512,1536]{3,2,1,0:T(8,128)(2,1)} %get-tuple-element.90.refs_0_, bf16[2,2,512,1536]{3,2,1,0:T(8,128)(2,1)} %get-tuple-element.91.refs_1_, bf16[2,512,768]{2,1,0:T(8,128)(2,1)} %get-tuple-element.92.refs_2_, bf16[2,512,768]{2,1,0:T(8,128)(2,1)} %get-tuple-element.93.refs_3_, ...), custom_call_target="tpu_custom_call" | custom-call | flops 1 | bytes 1 | tf_op jit(solution)/shard_map/dense_weight_grads/pallas_call | solution.py:945
  318.9 17.8 %filter_modes_back.3 = (bf16[8,2,64,768]{3,2,1,0:T(8,128)(2,1)}, f32[2,8,768]{2,1,0:T(8,128)}, f32[4,4,96,96]{3,2,1,0:T(8,128)}, f32[4,4,96,96]{3,2,1,0:T(8,128)}) custom-call(s32[6]{0:T(128)} %pad_add_fusion.limits.refs_0_, bf16[8,2,64,768]{3,2,1,0:T(8,128)(2,1)} %all-to-all-done.5.refs_10_.refs_1_.__1_.__2_, ...), custom_call_target="tpu_custom_call" | custom-call | flops 199999995904 | bytes 1 | tf_op jit(solution)/shard_map/filter_modes_back/pallas_call | solution.py:832
  336.6 3.5 all-to-all-done.6.__1_.spread
  340.1 4.7 %all-to-all-start.7 = ((bf16[8,2,64,768]{3,2,1,0:T(8,128)(2,1)}), bf16[8,2,64,768]{3,2,1,0:T(8,128)(2,1)}, u32[]{:S(2)}, u32[]{:S(2)}) async-start(bf16[8,2,64,768]{3,2,1,0:T(8,128)(2,1)} %tie.20), calls=%async_computation.7 | async-start | bytes 3145728 | tf_op jit(solution)/shard_map/all_to_all | solution.py:739
  346.0 1.3 collective-permute-done.3.refs_1_
  347.3 0.9 copy-done.6
  348.1 2.3 sum_and_cut.2
  350.5 1.5 collective-permute-start.4
  352.0 1.6 collective-permute-start.5
  354.0 0.8 slice_add_fusion
  354.9 1.3 concatenate.7.rest_0_.early
  356.1 2.5 collective-permute-done.4.refs_1_
  358.6 4.8 %collective-permute-done.5.refs_2_ = f32[4,96,96]{2,1,0:T(8,128)S(1)} collective-permute-done((f32[4,96,96]{2,1,0:T(8,128)}, f32[4,96,96]{2,1,0:T(8,128)S(1)}, u32[]{:S(2)}, u32[]{:S(2)}) %collective-permute-start.5) | collective-permute-done | bytes 147488 | tf_op jit(solution)/shard_map/ppermute | solution.py:167
  364.2 1.9 sum_and_cut.3
  366.1 5.9 %input_grads.2 = (bf16[4,1,1,512,768]{4,3,2,1,0:T(8,128)(2,1)}, f32[8,768]{1,0:T(8,128)}) custom-call(s32[6]{0:T(128)} %pad_add_fusion.limits.refs_0_, bf16[4,1,1,512,768]{4,3,2,1,0:T(8,128)(2,1)} %patches.7, bf16[8,2,64,768]{3,2,1,0:T(8,128)(2,1)} %all-to-all-done.6.__1_.spread, bf16[512,512]{1,0:T(8,128)(2,1)} %constant.35.clone.table_turned, ...), custom_call_target="tpu_custom_call" | custom-call | flops 805306368 | bytes 8650752 | tf_op jit(solution)/shard_map/input_grads/pallas_call | solution.py:961
  372.0 10.6 %all-to-all-done.7.spread.__1_ = bf16[8,2,64,768]{3,2,1,0:T(8,128)(2,1)} async-done(((bf16[8,2,64,768]{3,2,1,0:T(8,128)(2,1)}), bf16[8,2,64,768]{3,2,1,0:T(8,128)(2,1)}, u32[]{:S(2)}, u32[]{:S(2)}) %all-to-all-start.7) | async-done | bytes 1572896 | tf_op jit(solution)/shard_map/all_to_all | solution.py:739
  383.5 1.8 collective-permute-start.8
  385.3 2.6 collective-permute-start.9
  387.9 1.0 collective-permute-done.8
  388.8 2.4 collective-permute-done.9
  391.4 3.9 collective-permute-start.11
  396.4 5.9 %input_grads.3 = (bf16[4,1,1,512,768]{4,3,2,1,0:T(8,128)(2,1)}, f32[8,768]{1,0:T(8,128)}) custom-call(s32[6]{0:T(128)} %pad_add_fusion.limits.refs_0_, bf16[4,1,1,512,768]{4,3,2,1,0:T(8,128)(2,1)} %patches.7, bf16[8,2,64,768]{3,2,1,0:T(8,128)(2,1)} %all-to-all-done.7.spread.__1_, ...), custom_call_target="tpu_custom_call", output_to_operand_aliasing={{0}: (7, {})} | custom-call | flops 805306368 | bytes 8650752 | tf_op jit(solution)/shard_map/input_grads/pallas_call | solution.py:961
  403.0 1.6 place_blocks.2.refs_0_
  404.5 1.5 collective-permute-start.13
  406.0 1.6 collective-permute-start.14
  408.0 3.7 collective-permute-done.13.refs_1_
  411.8 3.4 collective-permute-done.14.refs_2_
  416.5 2.2 place_blocks.3.__1_.refs_4_
  418.7 1.7 pack_sums.1
  420.9 0.9 collective-permute-done.16
  421.8 0.8 add.75
  422.9 1.4 collective-permute-start.18
  424.4 1.8 collective-permute-start.19
  426.1 0.8 collective-permute-done.17
  427.0 2.3 collective-permute-done.19
  429.4 3.3 collective-permute-start.20
  432.8 2.3 collective-permute-start.22
  435.1 2.6 collective-permute-done.21
  437.7 1.1 collective-permute-done.22
  439.5 0.9 copy-done.5
  440.4 9.0 %update.1 = (f32[1,1]{1,0:T(1,128)}, f32[96,2,768]{2,1,0:T(2,128)}, f32[96,2,768]{2,1,0:T(2,128)}, f32[96,2,768]{2,1,0:T(2,128)}, f32[96,2,768]{2,1,0:T(2,128)},...) custom-call(f32[16,768]{1,0:T(8,128)} %add_add_fusion.late, ...), custom_call_target="tpu_custom_call" | custom-call | bytes 14155776 | tf_op jit(solution)/shard_map/update/pallas_call | solution.py:586
  (134 shorter events, 13.5 us)
Async XLA Ops:
  12.1 6.5 %copy-start.2 = (f32[96,2,768]{2,1,0:T(2,128)S(1)}, f32[96,2,768]{2,1,0:T(2,128)}, u32[]{:S(2)}) copy-start(f32[96,2,768]{2,1,0:T(2,128)} %refs_1_.1) | copy-start | bytes 1769476
  12.1 63.4 %all-to-all-start = ((bf16[8,2,64,768]{3,2,1,0:T(8,128)(2,1)}), bf16[8,2,64,768]{3,2,1,0:T(8,128)(2,1)}, u32[]{:S(2)}, u32[]{:S(2)}) async-start(bf16[8,2,64,768]{3,2,1,0:T(8,128)(2,1)} %get-tuple-element.78), calls=%async_computation | async-start | bytes 3145728 | tf_op jit(solution)/shard_map/all_to_all | solution.py:739
  18.6 56.0 %all-gather.3.cloned.1.call-start = ((), (), s32[]{:S(2)}) async-start(), calls=%async_computation.10 | async-start | bytes 1474560 | tf_op jit(solution)/shard_map/all_gather | solution.py:725
  19.4 140.6 %all-gather.5.cloned.1.call-start = ((), (), s32[]{:S(2)}) async-start(), calls=%async_computation.11 | async-start | bytes 5898240 | tf_op jit(solution)/shard_map/all_gather | solution.py:993
  75.5 4.5 copy-start.3
  75.6 5.2 %copy-start.1 = (f32[2,2,8,96,96]{4,3,2,1,0:T(8,128)S(1)}, f32[2,2,8,96,96]{4,3,2,1,0:T(8,128)}, u32[]{:S(2)}) copy-start(f32[2,2,8,96,96]{4,3,2,1,0:T(8,128)} %spectral.1) | copy-start | bytes 3538948
  75.6 42.3 %all-to-all-start.1 = ((bf16[8,2,64,768]{3,2,1,0:T(8,128)(2,1)}), bf16[8,2,64,768]{3,2,1,0:T(8,128)(2,1)}, u32[]{:S(2)}, u32[]{:S(2)}) async-start(bf16[8,2,64,768]{3,2,1,0:T(8,128)(2,1)} %tie.12), calls=%async_computation.1 | async-start | bytes 3145728 | tf_op jit(solution)/shard_map/all_to_all | solution.py:739
  80.7 3.1 copy-start.27
  80.7 4.4 copy-start.22
  80.7 4.4 copy-start.23
  81.6 2.2 copy-start
  117.9 42.1 %all-to-all-start.2 = ((bf16[8,2,64,768]{3,2,1,0:T(8,128)(2,1)}), bf16[8,2,64,768]{3,2,1,0:T(8,128)(2,1)}, u32[]{:S(2)}, u32[]{:S(2)}) async-start(bf16[8,2,64,768]{3,2,1,0:T(8,128)(2,1)} %tie.13), calls=%async_computation.2 | async-start | bytes 3145728 | tf_op jit(solution)/shard_map/all_to_all | solution.py:739
  160.0 8.3 %collective-permute-start = (bf16[2,1536,768]{2,1,0:T(8,128)(2,1)}, bf16[2,1536,768]{2,1,0:T(8,128)(2,1)}, u32[]{:S(2)}, u32[]{:S(2)}) collective-permute-start(bf16[2,1536,768]{2,1,0:T(8,128)(2,1)} %tie.16.mine), channel_id=1, source_target_pairs={{0,1},{1,0},{2,3},{3,2},{4,5},{5,4},{6,7},{7,6},{8,9},{9,8},{10,11... | collective-permute-start | bytes 14155784 | tf_op jit(solution)/shard_map/ppermute | solution.py:167
  160.0 45.3 %all-to-all-start.3 = ((bf16[8,2,64,768]{3,2,1,0:T(8,128)(2,1)}), bf16[8,2,64,768]{3,2,1,0:T(8,128)(2,1)}, u32[]{:S(2)}, u32[]{:S(2)}) async-start(bf16[8,2,64,768]{3,2,1,0:T(8,128)(2,1)} %tie.14), calls=%async_computation.3 | async-start | bytes 3145728 | tf_op jit(solution)/shard_map/all_to_all | solution.py:739
  205.3 42.2 %all-to-all-start.4 = ((bf16[8,2,64,768]{3,2,1,0:T(8,128)(2,1)}), bf16[8,2,64,768]{3,2,1,0:T(8,128)(2,1)}, u32[]{:S(2)}, u32[]{:S(2)}) async-start(bf16[8,2,64,768]{3,2,1,0:T(8,128)(2,1)} %tie.17), calls=%async_computation.4 | async-start | bytes 3145728 | tf_op jit(solution)/shard_map/all_to_all | solution.py:739
  247.5 50.5 %all-to-all-start.5 = ((bf16[8,2,64,768]{3,2,1,0:T(8,128)(2,1)}), bf16[8,2,64,768]{3,2,1,0:T(8,128)(2,1)}, u32[]{:S(2)}, u32[]{:S(2)}) async-start(bf16[8,2,64,768]{3,2,1,0:T(8,128)(2,1)} %tie.18), calls=%async_computation.5 | async-start | bytes 3145728 | tf_op jit(solution)/shard_map/all_to_all | solution.py:739
  291.4 11.1 %collective-permute-start.1 = (bf16[1536,768]{1,0:T(8,128)(2,1)}, bf16[1536,768]{1,0:T(8,128)(2,1)}, u32[]{:S(2)}, u32[]{:S(2)}) collective-permute-start(bf16[1536,768]{1,0:T(8,128)(2,1)} %get-tuple-element.98), channel_id=1, source_target_pairs={{0,1},{1,0},{2,3},{3,2},{4,5},{5,4},{6,7},{7,6},{8,9},{9,8},{10,11... | collective-permute-start | bytes 7077896 | tf_op jit(solution)/shard_map/ppermute | solution.py:167
  291.7 10.8 %collective-permute-start.2 = (bf16[1536,768]{1,0:T(8,128)(2,1)}, bf16[1536,768]{1,0:T(8,128)(2,1)}, u32[]{:S(2)}, u32[]{:S(2)}) collective-permute-start(bf16[1536,768]{1,0:T(8,128)(2,1)} %get-tuple-element.99), channel_id=1, source_target_pairs={{0,1},{1,0},{2,3},{3,2},{4,5},{5,4},{6,7},{7,6},{8,9},{9,8},{10,11... | collective-permute-start | bytes 7077896 | tf_op jit(solution)/shard_map/ppermute | solution.py:167
  298.0 42.1 %all-to-all-start.6 = ((bf16[8,2,64,768]{3,2,1,0:T(8,128)(2,1)}), bf16[8,2,64,768]{3,2,1,0:T(8,128)(2,1)}, u32[]{:S(2)}, u32[]{:S(2)}) async-start(bf16[8,2,64,768]{3,2,1,0:T(8,128)(2,1)} %tie.19), calls=%async_computation.6 | async-start | bytes 3145728 | tf_op jit(solution)/shard_map/all_to_all | solution.py:739
  302.3 80.4 %reduce-scatter.3.cloned.1.call-start = ((), (), s32[]{:S(2)}) async-start(), calls=%async_computation.12 | async-start | bytes 5898240 | tf_op jit(solution)/shard_map/reduce_scatter | solution.py:1015
  340.1 4.8 %copy-start.24 = (f32[4,4,96,96]{3,2,1,0:T(8,128)S(1)}, f32[4,4,96,96]{3,2,1,0:T(8,128)}, u32[]{:S(2)}) copy-start(f32[4,4,96,96]{3,2,1,0:T(8,128)} %get-tuple-element.104) | copy-start | bytes 1769476
  340.1 5.2 %copy-start.20 = (f32[8,768]{1,0:T(8,128)S(1)}, f32[8,768]{1,0:T(8,128)}, u32[]{:S(2)}) copy-start(f32[8,768]{1,0:T(8,128)} %get-tuple-element.114) | copy-start | bytes 73732
  340.1 5.2 %copy-start.21 = (f32[8,768]{1,0:T(8,128)S(1)}, f32[8,768]{1,0:T(8,128)}, u32[]{:S(2)}) copy-start(f32[8,768]{1,0:T(8,128)} %get-tuple-element.115) | copy-start | bytes 73732
  340.1 5.2 %copy-start.19 = (f32[2,2,1,1536]{3,2,1,0:T(1,128)S(1)}, f32[2,2,1,1536]{3,2,1,0:T(1,128)}, u32[]{:S(2)}) copy-start(f32[2,2,1,1536]{3,2,1,0:T(1,128)} %get-tuple-element.119) | copy-start | bytes 73732
  340.1 5.3 %copy-start.18 = (f32[2,2,1,1536]{3,2,1,0:T(1,128)S(1)}, f32[2,2,1,1536]{3,2,1,0:T(1,128)}, u32[]{:S(2)}) copy-start(f32[2,2,1,1536]{3,2,1,0:T(1,128)} %get-tuple-element.118) | copy-start | bytes 73732
  340.1 42.5 %all-to-all-start.7 = ((bf16[8,2,64,768]{3,2,1,0:T(8,128)(2,1)}), bf16[8,2,64,768]{3,2,1,0:T(8,128)(2,1)}, u32[]{:S(2)}, u32[]{:S(2)}) async-start(bf16[8,2,64,768]{3,2,1,0:T(8,128)(2,1)} %tie.20), calls=%async_computation.7 | async-start | bytes 3145728 | tf_op jit(solution)/shard_map/all_to_all | solution.py:739
  344.8 73.9 %reduce-scatter.5.cloned.1.call-start = ((), (), s32[]{:S(2)}) async-start(), calls=%async_computation.13 | async-start | bytes 1474560 | tf_op jit(solution)/shard_map/reduce_scatter | solution.py:1038
  344.9 2.4 collective-permute-start.3
  347.3 0.9 copy-start.6
  350.5 8.2 %collective-permute-start.4 = (f32[4,96,96]{2,1,0:T(8,128)}, f32[4,96,96]{2,1,0:T(8,128)S(1)}, u32[]{:S(2)}, u32[]{:S(2)}) collective-permute-start(f32[4,96,96]{2,1,0:T(8,128)} %get-tuple-element.106), channel_id=1, source_target_pairs={{0,8},{8,0},{16,24},{24,16},{1,9},{9,1},{17,25},{25,17},{2,10},{10... | collective-permute-start | bytes 442376 | tf_op jit(solution)/shard_map/ppermute | solution.py:167
  352.0 11.5 %collective-permute-start.5 = (f32[4,96,96]{2,1,0:T(8,128)}, f32[4,96,96]{2,1,0:T(8,128)S(1)}, u32[]{:S(2)}, u32[]{:S(2)}) collective-permute-start(f32[4,96,96]{2,1,0:T(8,128)} %get-tuple-element.107), channel_id=1, source_target_pairs={{0,16},{8,24},{16,0},{24,8},{1,17},{9,25},{17,1},{25,9},{2,18},{10... | collective-permute-start | bytes 442376 | tf_op jit(solution)/shard_map/ppermute | solution.py:167
  353.6 10.0 %collective-permute-start.6 = (f32[4,96,96]{2,1,0:T(8,128)}, f32[4,96,96]{2,1,0:T(8,128)S(1)}, u32[]{:S(2)}, u32[]{:S(2)}) collective-permute-start(f32[4,96,96]{2,1,0:T(8,128)} %get-tuple-element.108), channel_id=1, source_target_pairs={{0,24},{8,16},{16,8},{24,0},{1,25},{9,17},{17,9},{25,1},{2,26},{10... | collective-permute-start | bytes 442376 | tf_op jit(solution)/shard_map/ppermute | solution.py:167
  358.6 4.9 %copy-start.10 = (f32[4,96,96]{2,1,0:T(8,128)}, f32[4,96,96]{2,1,0:T(8,128)S(1)}, u32[]{:S(2)}) copy-start(f32[4,96,96]{2,1,0:T(8,128)S(1)} %collective-permute-done.4.refs_1_) | copy-start | bytes 442372
  363.5 0.7 copy-start.11
  363.5 0.7 copy-start.12
  382.7 0.8 copy-start.26
  382.7 0.8 copy-start.25
  382.7 2.6 copy-start.13
  382.7 8.6 %copy-start.17 = (f32[96,96]{1,0:T(8,128)S(1)}, f32[96,96]{1,0:T(8,128)}, u32[]{:S(2)}) copy-start(f32[96,96]{1,0:T(8,128)} %get-tuple-element.109) | copy-start | bytes 110596
  383.5 4.4 collective-permute-start.7
  383.5 5.3 %collective-permute-start.8 = (f32[96,96]{1,0:T(8,128)S(1)}, f32[96,96]{1,0:T(8,128)S(1)}, u32[]{:S(2)}, u32[]{:S(2)}) collective-permute-start(f32[96,96]{1,0:T(8,128)S(1)} %copy-done.25), channel_id=1, source_target_pairs={{0,4},{1,5},{2,6},{3,7},{4,0},{5,1},{6,2},{7,3},{8,12},{9,13},{10,... | collective-permute-start | bytes 110600 | tf_op jit(solution)/shard_map/ppermute | solution.py:167
  385.3 6.0 %collective-permute-start.9 = (f32[96,96]{1,0:T(8,128)S(1)}, f32[96,96]{1,0:T(8,128)S(1)}, u32[]{:S(2)}, u32[]{:S(2)}) collective-permute-start(f32[96,96]{1,0:T(8,128)S(1)} %copy-done.13), channel_id=1, source_target_pairs={{0,6},{1,7},{2,4},{3,5},{4,2},{5,3},{6,0},{7,1},{8,14},{9,15},{10,... | collective-permute-start | bytes 110600 | tf_op jit(solution)/shard_map/ppermute | solution.py:167
  391.3 5.1 %copy-start.4 = (f32[96,96]{1,0:T(8,128)}, f32[96,96]{1,0:T(8,128)S(1)}, u32[]{:S(2)}) copy-start(f32[96,96]{1,0:T(8,128)S(1)} %add_add_fusion.2.rest_0_.__0_) | copy-start | bytes 110596
  391.3 11.0 %collective-permute-start.10 = (f32[96,96]{1,0:T(8,128)S(1)}, f32[96,96]{1,0:T(8,128)S(1)}, u32[]{:S(2)}, u32[]{:S(2)}) collective-permute-start(f32[96,96]{1,0:T(8,128)S(1)} %add_add_fusion.2.rest_0_.__0_), channel_id=1, source_target_pairs={{0,2},{1,3},{2,0},{3,1},{4,6},{5,7},{6,4},{7,5},{8,10},{9,11},{10,... | collective-permute-start | bytes 110600 | tf_op jit(solution)/shard_map/ppermute | solution.py:167
  391.4 10.9 %collective-permute-start.11 = (f32[96,96]{1,0:T(8,128)S(1)}, f32[96,96]{1,0:T(8,128)S(1)}, u32[]{:S(2)}, u32[]{:S(2)}) collective-permute-start(f32[96,96]{1,0:T(8,128)S(1)} %add_add_fusion.2.rest_0_.__0_), channel_id=1, source_target_pairs={{0,4},{1,5},{2,6},{3,7},{4,0},{5,1},{6,2},{7,3},{8,12},{9,13},{10,... | collective-permute-start | bytes 110600 | tf_op jit(solution)/shard_map/ppermute | solution.py:167
  395.3 7.0 %collective-permute-start.12 = (f32[96,96]{1,0:T(8,128)S(1)}, f32[96,96]{1,0:T(8,128)S(1)}, u32[]{:S(2)}, u32[]{:S(2)}) collective-permute-start(f32[96,96]{1,0:T(8,128)S(1)} %add_add_fusion.2.rest_0_.__0_), channel_id=1, source_target_pairs={{0,6},{1,7},{2,4},{3,5},{4,2},{5,3},{6,0},{7,1},{8,14},{9,15},{10,... | collective-permute-start | bytes 110600 | tf_op jit(solution)/shard_map/ppermute | solution.py:167
  402.3 0.6 copy-start.14
  402.3 0.6 copy-start.15
  402.3 0.6 copy-start.16
  404.5 7.2 %collective-permute-start.13 = (f32[4,96,96]{2,1,0:T(8,128)}, f32[4,96,96]{2,1,0:T(8,128)S(1)}, u32[]{:S(2)}, u32[]{:S(2)}) collective-permute-start(f32[4,96,96]{2,1,0:T(8,128)} %place_blocks.2.refs_0_), channel_id=1, source_target_pairs={{0,8},{8,0},{16,24},{24,16},{1,9},{9,1},{17,25},{25,17},{2,10},{10... | collective-permute-start | bytes 442376 | tf_op jit(solution)/shard_map/ppermute | solution.py:167
  406.0 9.2 %collective-permute-start.14 = (f32[4,96,96]{2,1,0:T(8,128)}, f32[4,96,96]{2,1,0:T(8,128)S(1)}, u32[]{:S(2)}, u32[]{:S(2)}) collective-permute-start(f32[4,96,96]{2,1,0:T(8,128)} %place_blocks.2.refs_0_), channel_id=1, source_target_pairs={{0,16},{8,24},{16,0},{24,8},{1,17},{9,25},{17,1},{25,9},{2,18},{10... | collective-permute-start | bytes 442376 | tf_op jit(solution)/shard_map/ppermute | solution.py:167
  407.6 7.6 %collective-permute-start.15 = (f32[4,96,96]{2,1,0:T(8,128)}, f32[4,96,96]{2,1,0:T(8,128)S(1)}, u32[]{:S(2)}, u32[]{:S(2)}) collective-permute-start(f32[4,96,96]{2,1,0:T(8,128)} %place_blocks.2.refs_0_), channel_id=1, source_target_pairs={{0,24},{8,16},{16,8},{24,0},{1,25},{9,17},{17,9},{25,1},{2,26},{10... | collective-permute-start | bytes 442376 | tf_op jit(solution)/shard_map/ppermute | solution.py:167
  411.8 3.4 copy-start.7
  415.2 0.7 copy-start.8
  415.8 0.7 copy-start.9
  420.4 1.4 collective-permute-start.16
  420.4 19.0 %collective-permute-start.23 = (f32[4,4,96,96]{3,2,1,0:T(8,128)}, f32[4,4,96,96]{3,2,1,0:T(8,128)S(1)}, u32[]{:S(2)}, u32[]{:S(2)}) collective-permute-start(f32[4,4,96,96]{3,2,1,0:T(8,128)} %place_blocks.3.__1_.refs_4_), channel_id=1, source_target_pairs={{0,1},{1,0},{2,3},{3,2},{4,5},{5,4},{6,7},{7,6},{8,9},{9,8},{10,11... | collective-permute-start | bytes 1769480 | tf_op jit(solution)/shard_map/ppermute | solution.py:167
  422.7 4.3 collective-permute-start.17
  422.9 4.1 collective-permute-start.18
  424.4 5.0 %collective-permute-start.19 = (f32[16,768]{1,0:T(8,128)S(1)}, f32[16,768]{1,0:T(8,128)S(1)}, u32[]{:S(2)}, u32[]{:S(2)}) collective-permute-start(f32[16,768]{1,0:T(8,128)S(1)} %add.75), channel_id=1, source_target_pairs={{0,24},{8,16},{16,8},{24,0},{1,25},{9,17},{17,9},{25,1},{2,26},{10... | collective-permute-start | bytes 147464 | tf_op jit(solution)/shard_map/ppermute | solution.py:167
  429.4 5.8 %collective-permute-start.20 = (f32[16,768]{1,0:T(8,128)S(1)}, f32[16,768]{1,0:T(8,128)S(1)}, u32[]{:S(2)}, u32[]{:S(2)}) collective-permute-start(f32[16,768]{1,0:T(8,128)S(1)} %add_add_fusion.1), channel_id=1, source_target_pairs={{0,2},{1,3},{2,0},{3,1},{4,6},{5,7},{6,4},{7,5},{8,10},{9,11},{10,... | collective-permute-start | bytes 147464 | tf_op jit(solution)/shard_map/ppermute | solution.py:167
  432.7 5.0 %collective-permute-start.21 = (f32[16,768]{1,0:T(8,128)S(1)}, f32[16,768]{1,0:T(8,128)S(1)}, u32[]{:S(2)}, u32[]{:S(2)}) collective-permute-start(f32[16,768]{1,0:T(8,128)S(1)} %add_add_fusion.1), channel_id=1, source_target_pairs={{0,4},{1,5},{2,6},{3,7},{4,0},{5,1},{6,2},{7,3},{8,12},{9,13},{10,... | collective-permute-start | bytes 147464 | tf_op jit(solution)/shard_map/ppermute | solution.py:167
  432.8 6.0 %collective-permute-start.22 = (f32[16,768]{1,0:T(8,128)S(1)}, f32[16,768]{1,0:T(8,128)S(1)}, u32[]{:S(2)}, u32[]{:S(2)}) collective-permute-start(f32[16,768]{1,0:T(8,128)S(1)} %add_add_fusion.1), channel_id=1, source_target_pairs={{0,6},{1,7},{2,4},{3,5},{4,2},{5,3},{6,0},{7,1},{8,14},{9,15},{10,... | collective-permute-start | bytes 147464 | tf_op jit(solution)/shard_map/ppermute | solution.py:167
  439.5 0.9 copy-start.5
Sparse Core Ops, SparseCore 0:
  21.6 52.9 all-gather.2
  76.4 55.2 all-gather.4
  319.0 58.6 reduce-scatter.2
  382.8 31.2 reduce-scatter.4
